TPU v7x, 128 devices: a whole 4x4x4 slice. The times are simulated.
128 devices in a mesh: dyn: 8 (over x, core), col: 16 (over z, y).
Axes of the slice: x: 4, y: 4, z: 4, core: 2. Of those that a mesh axis runs over, the one named last changes fastest.
Arguments:
- planck_source: float32 [32, 131072], P(None, ('dyn', 'col')), may hold values from 0.5 to 1.5
- absorber_path: float32 [32, 131072], P(None, ('dyn', 'col')), may hold values from 0.2 to 3
- cloud_depth: float32 [32, 131072], P(None, ('dyn', 'col')), may hold values from 0 to 0.6
- span_map: int32 [131072], P(('dyn', 'col')), may hold values from 0 to 131071, as said below
- surface_source: float32 [131072], P(('dyn', 'col')), may hold values from 0.8 to 1.6
- interp_index: int32 [32, 131072], P(None, ('dyn', 'col')), may hold values from 0 to 830
- interp_weight: bfloat16 [4, 32, 131072], P(None, None, ('dyn', 'col')), may hold values from 0 to 0.5
- sunlit: int32 [131072], P(('dyn', 'col')), may hold values from 0 to 1, as said below
- sw_slot: int32 [131072], P(('dyn', 'col')), may hold values from 0 to 8191, as said below
- cos_zenith: float32 [131072], P(('dyn', 'col')), may hold values from 0.05 to 1
- albedo: float32 [131072], P(('dyn', 'col')), may hold values from 0.05 to 0.8
- table_lw: bfloat16 [256, 896], replicated, may hold values from 0.0029907227 to 3
- table_sw: bfloat16 [224, 896], replicated, may hold values from 0.0029 to 3
- planck_frac: float32 [256], replicated, may hold values from 0.0001 to 0.02
- solar_weight: float32 [224], replicated, may hold values from 0.0001 to 0.02
Outputs:
- heating_lw: float32 [32, 131072], P(None, ('dyn', 'col'))
- heating_sw: float32 [32, 131072], P(None, ('dyn', 'col'))
- sw_surface: float32 [65536], P(('dyn', 'col'))
Inputs may be any that keep to these rules, and one draw needn't show every extreme that they name: A permutation of the 131072 physics columns: column i goes to device span_map[i] // 1024 (flat index dyn * 16 + col), position span_map[i] % 1024. The number of columns that device s sends to device t depends only on (t - s) modulo the number of devices, is at most 16, and equals 16 for some pairs. In each dyn row the devices fall into pairs whose sunlit counts add up to 1024, so a dyn row holds 8192 sunlit columns; in every dyn row some device is sunlit in all its columns. For a sunlit column, sw_slot // 512 is the col index of the device of its dyn row that computes its shortwave and sw_slot % 512 its slot there. The sunlit columns of a dyn row, in order of device and column, are dealt to owners in turn from a drawn start; the values are distinct, every owner gets exactly 512, at most 64 from any one device and exactly that many from a fully sunlit one. For dark columns the value is arbitrary.
All inputs are finite; a program needn't handle non-finite values.
Results may differ from a plain program's by a relative error of at most 0.0003.
Values may be sent and summed in bfloat16 or wider, within the bound.
No kernel may reach another device: no remote copies, remote signals or barrier semaphores. Data moves between devices by JAX's collectives and lax.ppermute only.
A program may use at most 128 MiB of HBM per device.

v0:
```python
from functools import partial

import jax
import jax.numpy as jnp
from jax import lax
from jax.sharding import PartitionSpec as P

TEMPS = 14
PRESS = 64


def corner_weights(index_row, weight_rows):
    entries = jnp.arange(TEMPS * PRESS, dtype=jnp.int32)[:, None]
    offsets = (0, 1, PRESS, PRESS + 1)
    mixing = jnp.zeros((TEMPS * PRESS, index_row.shape[0]), jnp.bfloat16)
    for corner in range(4):
        matches = entries == index_row[None, :] + offsets[corner]
        mixing = mixing + jnp.where(
            matches, weight_rows[corner][None, :], jnp.zeros((), jnp.bfloat16)
        )
    return mixing


def optical_depth(table, index_row, weight_rows, path_row, cloud_row):
    absorb = jnp.dot(
        table, corner_weights(index_row, weight_rows), preferred_element_type=jnp.float32
    )
    return path_row[None, :] * absorb + cloud_row[None, :]


def longwave(
    table, planck_frac, index_cols, weight_cols, path_cols, cloud_cols, planck_cols, surface_cols
):
    fraction = planck_frac[:, None]
    weight_levels = jnp.moveaxis(weight_cols, 0, 1)

    def longwave_downward(flux_in, inputs):
        index_row, weight_rows, path_row, cloud_row, planck_row = inputs
        optical = optical_depth(table, index_row, weight_rows, path_row, cloud_row)
        transmit = jnp.exp(-1.66 * optical)
        flux_out = flux_in * transmit + fraction * planck_row[None, :] * (1.0 - transmit)
        return (flux_out, (transmit, jnp.sum(flux_in - flux_out, axis=0)))

    initial = jnp.zeros((table.shape[0], index_cols.shape[1]), jnp.float32)
    bottom_down, (transmits, gained_down) = lax.scan(
        longwave_downward, initial, (index_cols, weight_levels, path_cols, cloud_cols, planck_cols)
    )

    def longwave_upward(flux_in, inputs):
        transmit, planck_row = inputs
        flux_out = flux_in * transmit + fraction * planck_row[None, :] * (1.0 - transmit)
        return (flux_out, jnp.sum(flux_in - flux_out, axis=0))

    ground = fraction * surface_cols[None, :]
    top_up, gained_up = lax.scan(longwave_upward, ground, (transmits, planck_cols), reverse=True)
    return gained_down + gained_up


def shortwave(
    table, solar_weight, index_cols, weight_cols, path_cols, cloud_cols, cosine_cols, albedo_cols
):
    weight_levels = jnp.moveaxis(weight_cols, 0, 1)

    def shortwave_downward(beam_in, inputs):
        index_row, weight_rows, path_row, cloud_row = inputs
        optical = optical_depth(table, index_row, weight_rows, path_row, cloud_row)
        beam_out = beam_in * jnp.exp(-optical / cosine_cols[None, :])
        return (beam_out, (jnp.exp(-1.66 * optical), jnp.sum(beam_in - beam_out, axis=0)))

    initial = solar_weight[:, None] * cosine_cols[None, :]
    ground_beam, (diffuse, gained_down) = lax.scan(
        shortwave_downward, initial, (index_cols, weight_levels, path_cols, cloud_cols)
    )

    def shortwave_upward(flux_in, transmit):
        flux_out = flux_in * transmit
        return (flux_out, jnp.sum(flux_in - flux_out, axis=0))

    top_up, gained_up = lax.scan(
        shortwave_upward, albedo_cols[None, :] * ground_beam, diffuse, reverse=True
    )
    ground_gain = jnp.sum(ground_beam, axis=0) * (1.0 - albedo_cols)
    return (gained_down + gained_up, ground_gain)


def by_blocks(function, arrays, block_cols):
    block_count = arrays[0].shape[-1] // block_cols

    def to_blocks(values):
        shaped = values.reshape(values.shape[:-1] + (block_count, block_cols))
        return jnp.moveaxis(shaped, -2, 0)

    def from_blocks(values):
        joined = jnp.moveaxis(values, 0, -2)
        return joined.reshape(joined.shape[:-2] + (block_count * block_cols,))

    results = lax.map(
        lambda block_args: function(*block_args), tuple((to_blocks(values) for values in arrays))
    )
    return jax.tree.map(from_blocks, results)


def deal_slots(holder, parties, capacity, columns):
    marked = (holder[:, None] == jnp.arange(parties, dtype=jnp.int32)[None, :]).astype(jnp.int32)
    placed = jnp.sum(jnp.cumsum(marked, axis=0) * marked, axis=1) - 1
    position = jnp.where(holder < parties, holder * capacity + placed, parties * capacity)
    filler = (
        jnp.full((parties * capacity,), columns, jnp.int32)
        .at[position]
        .set(jnp.arange(columns, dtype=jnp.int32), mode="drop")
    )
    return (position, filler)


def gather_cols(values, index, blank):
    return jnp.take(values, index, axis=-1, mode="fill", fill_value=blank)


def body(
    planck_source,
    absorber_path,
    cloud_depth,
    span_map,
    surface_source,
    interp_index,
    interp_weight,
    sunlit,
    sw_slot,
    cos_zenith,
    albedo,
    table_lw,
    table_sw,
    planck_frac,
    solar_weight,
):
    columns = span_map.shape[0]
    groups = lax.axis_size("dyn")
    devices = groups * lax.axis_size("col")
    capacity = 2 * columns // devices
    slots = devices * capacity
    position, filler = deal_slots(span_map // columns, devices, capacity, columns)
    planck_out = gather_cols(planck_source, filler, 0.0)
    path_out = gather_cols(absorber_path, filler, 0.0)
    cloud_out = gather_cols(cloud_depth, filler, 0.0)
    label_out = gather_cols(span_map % columns, filler, columns)[None, :].astype(jnp.float32)
    planck_in, path_in, cloud_in, label_in = (
        lax.all_to_all(planck_out, ("dyn", "col"), split_axis=1, concat_axis=1, tiled=True),
        lax.all_to_all(path_out, ("dyn", "col"), split_axis=1, concat_axis=1, tiled=True),
        lax.all_to_all(cloud_out, ("dyn", "col"), split_axis=1, concat_axis=1, tiled=True),
        lax.all_to_all(label_out, ("dyn", "col"), split_axis=1, concat_axis=1, tiled=True),
    )
    landing = label_in[0].astype(jnp.int32)
    anchor = (
        jnp.full((columns,), slots, jnp.int32)
        .at[landing]
        .set(jnp.arange(slots, dtype=jnp.int32), mode="drop")
    )
    planck_phys = jnp.take(planck_in, anchor, axis=1)
    path_phys = jnp.take(path_in, anchor, axis=1)
    cloud_phys = jnp.take(cloud_in, anchor, axis=1)
    block_cols = min(512, columns)
    lw_heat = by_blocks(
        partial(longwave, table_lw, planck_frac),
        (interp_index, interp_weight, path_phys, cloud_phys, planck_phys, surface_source),
        block_cols,
    )
    stripes = lax.axis_size("col")
    sw_count = columns // 2
    sw_capacity = columns // stripes
    holder = jnp.where(sunlit == 1, sw_slot // sw_count, stripes)
    sw_position, sw_filler = deal_slots(holder, stripes, sw_capacity, columns)
    sw_target = gather_cols(sw_slot % sw_count, sw_filler, sw_count)[None, :].astype(jnp.float32)
    levels = interp_index.shape[0]
    index_wide = interp_index.astype(jnp.float32)
    delivered = (
        lax.all_to_all(
            gather_cols(path_phys, sw_filler, 0.0), "col", split_axis=1, concat_axis=1, tiled=True
        ),
        lax.all_to_all(
            gather_cols(cloud_phys, sw_filler, 0.0), "col", split_axis=1, concat_axis=1, tiled=True
        ),
        lax.all_to_all(
            gather_cols(cos_zenith[None, :], sw_filler, 1.0),
            "col",
            split_axis=1,
            concat_axis=1,
            tiled=True,
        ),
        lax.all_to_all(
            gather_cols(albedo[None, :], sw_filler, 0.0),
            "col",
            split_axis=1,
            concat_axis=1,
            tiled=True,
        ),
        lax.all_to_all(
            gather_cols(index_wide, sw_filler, 0.0), "col", split_axis=1, concat_axis=1, tiled=True
        ),
        lax.all_to_all(sw_target, "col", split_axis=1, concat_axis=1, tiled=True),
    )
    weight_rows = interp_weight.reshape(4 * levels, columns)
    weight_in = lax.all_to_all(
        gather_cols(weight_rows, sw_filler, 0.0), "col", split_axis=1, concat_axis=1, tiled=True
    )
    arrival = delivered[5][0].astype(jnp.int32)
    compact = (
        jnp.full((sw_count,), columns, jnp.int32)
        .at[arrival]
        .set(jnp.arange(columns, dtype=jnp.int32), mode="drop")
    )
    path_sun, cloud_sun, cosine_sun, albedo_sun, index_sun = tuple(
        (jnp.take(values, compact, axis=1) for values in delivered[:5])
    )
    weight_sun = jnp.take(weight_in, compact, axis=1).reshape(4, levels, sw_count)
    index_sun = index_sun.astype(jnp.int32)
    sw_local, sw_surface = by_blocks(
        partial(shortwave, table_sw, solar_weight),
        (index_sun, weight_sun, path_sun, cloud_sun, cosine_sun[0], albedo_sun[0]),
        min(512, sw_count),
    )
    returned = lax.all_to_all(
        gather_cols(sw_local, arrival, 0.0), "col", split_axis=1, concat_axis=1, tiled=True
    )
    sw_heat = gather_cols(returned, sw_position, 0.0)
    lw_back = gather_cols(lw_heat, landing, 0.0)
    sw_back = gather_cols(sw_heat, landing, 0.0)
    lw_home, sw_home = (
        lax.all_to_all(lw_back, ("dyn", "col"), split_axis=1, concat_axis=1, tiled=True),
        lax.all_to_all(sw_back, ("dyn", "col"), split_axis=1, concat_axis=1, tiled=True),
    )
    heating_lw = jnp.take(lw_home, position, axis=1)
    heating_sw = jnp.take(sw_home, position, axis=1)
    return (heating_lw, heating_sw, sw_surface)


def solution(mesh):
    in_specs = (
        P(None, ("dyn", "col")),
        P(None, ("dyn", "col")),
        P(None, ("dyn", "col")),
        P(("dyn", "col")),
        P(("dyn", "col")),
        P(None, ("dyn", "col")),
        P(None, None, ("dyn", "col")),
        P(("dyn", "col")),
        P(("dyn", "col")),
        P(("dyn", "col")),
        P(("dyn", "col")),
        P(),
        P(),
        P(),
        P(),
    )
    out_specs = (P(None, ("dyn", "col")), P(None, ("dyn", "col")), P(("dyn", "col")))
    return jax.shard_map(body, mesh=mesh, in_specs=in_specs, out_specs=out_specs, check_vma=False)
```

profile of v0, /device:TPU:1, one launch (start us, length us, event | category | flops | bytes accessed | tf_op | source)
XLA Modules:
  0.0 820.8 jit_solution(1647245108805929346)
XLA Ops:
  21.6 8.6 %all-to-all-start.5 = ((f32[1,16,64]{2,0,1:T(1,128)}), f32[1,16,64]{2,0,1:T(1,128)S(1)}, u32[]{:S(2)}, u32[]{:S(2)}) async-start(f32[1,16,64]{2,0,1:T(1,128)} %reshape.630), calls=%async_computation.5 | async-start | bytes 16384 | tf_op jit(solution)/shard_map/all_to_all | solution.py:199
  42.1 7.6 gather_fusion.11
  49.7 8.6 %gather_fusion = s32[2048]{0:T(1024)S(1)} fusion(s32[1024]{0:T(1024)S(1)} %get-tuple-element.830, s32[2048]{0:T(1024)S(1)} %fusion.61), kind=kCustom, calls=%fused_computation.19 | custom fusion | bytes 24576 | tf_op jit(solution)/shard_map/jit(_take)/gather | solution.py:116
  59.1 7.6 gather_fusion.7
  66.9 7.6 gather_fusion.9
  95.3 6.7 all-to-all-start.6
  120.0 8.4 %all-to-all-start.1 = ((f32[1,128,16]{2,0,1:T(1,128)}), f32[1,128,16]{2,0,1:T(1,128)S(1)}, u32[]{:S(2)}, u32[]{:S(2)}) async-start(f32[1,128,16]{2,0,1:T(1,128)} %bitcast.29), calls=%async_computation.1 | async-start | bytes 131072 | tf_op jit(solution)/shard_map/all_to_all | solution.py:150
  146.8 7.0 all-to-all-done.3
  157.8 8.0 scatter_custom_fusion.1
  169.2 6.4 all-to-all-start
  187.4 7.3 all-to-all-start.9
  214.2 6.7 all-to-all-start.10
  251.7 102.0 %while.122 = (s32[]{:T(128)}, f32[224,512]{1,0:T(8,128)S(1)}, f32[32,224,512]{2,1,0:T(8,128)}, f32[32,512]{1,0:T(8,128)S(1)}, f32[32,512]{1,0:T(8,128)S(1)}, /*i...) while((s32[]{:T(128)}, f32[224,512]{1,0:T(8,128)S(1)}, ...), condition=%wide.region_20.26_spmd, body=%wide.region_18.25_spmd.sunk | while | flops 213779456 | bytes 2748633 | solution.py:71
  354.4 43.4 %while.123 = (s32[]{:T(128)}, f32[224,512]{1,0:T(8,128)S(1)}, f32[32,512]{1,0:T(8,128)S(1)}, f32[32,224,512]{2,1,0:T(8,128)}, s32[]{:T(128)}, /*index=5*/s32[]{:T(128)}, s32[]{:T(128)}) while((s32[]{:T(128)}, f32[224,512]{1,0:T(8,128)S(1)}, f32[32,512]{1,0:T(8,128)S(1)}, f32[32,224,512]{2,1,0:T(8,128)}, s32[]{:T(128)}, ...), condition=%wide.region_23.29_spmd, body=%wide.region_21.28_spmd.sunk | while | flops 343555 | bytes 1382505 | solution.py:79
  401.9 6.4 all-to-all-start.12
  408.4 343.0 %while.121 = (s32[]{:T(128)}, f32[2,32,512]{2,1,0:T(8,128)S(1)}, s32[2,32,512]{2,0,1:T(2,128)S(1)}, bf16[2,4,32,512]{3,1,2,0:T(4,128)(2,1)S(1)}, f32[2,32,512]{2...) while((s32[]{:T(128)}, f32[2,32,512]{2,1,0:T(8,128)S(1)}, ...), condition=%wide.region_12.15_spmd, body=%wide.region_5.14_spmd.sunk | while | flops 244728320 | bytes 6502201 | solution.py:97
  408.6 126.9 %while.124 = (s32[]{:T(128)}, f32[256,512]{1,0:T(8,128)}, f32[32,256,512]{2,1,0:T(8,128)}, f32[32,512]{1,0:T(8,128)S(1)}, f32[32,512]{1,0:T(8,128)S(1)}, /*index...) while((s32[]{:T(128)}, f32[256,512]{1,0:T(8,128)}, ...), condition=%wide.region_8.10_spmd.clone, body=%wide.region_6.9_spmd.clone.sunk | while | flops 243663872 | bytes 3138799 | solution.py:45
  535.6 44.2 %while.125 = (s32[]{:T(128)}, f32[256,512]{1,0:T(8,128)S(1)}, f32[32,512]{1,0:T(8,128)S(1)}, f32[32,256,512]{2,1,0:T(8,128)}, f32[256,1]{0,1:T(1,128)S(1)}, /*in...) while((s32[]{:T(128)}, f32[256,512]{1,0:T(8,128)S(1)}, f32[32,512]{1,0:T(8,128)S(1)}, ...), condition=%wide.region_11.13_spmd, body=%wide.region_9.12_spmd.sunk | while | flops 916995 | bytes 1586301 | solution.py:55
  580.1 126.9 %while.124 = (s32[]{:T(128)}, f32[256,512]{1,0:T(8,128)}, f32[32,256,512]{2,1,0:T(8,128)}, f32[32,512]{1,0:T(8,128)S(1)}, f32[32,512]{1,0:T(8,128)S(1)}, /*index...) while((s32[]{:T(128)}, f32[256,512]{1,0:T(8,128)}, ...), condition=%wide.region_8.10_spmd.clone, body=%wide.region_6.9_spmd.clone.sunk | while | flops 243663872 | bytes 3138799 | solution.py:45
  707.1 44.2 %while.125 = (s32[]{:T(128)}, f32[256,512]{1,0:T(8,128)S(1)}, f32[32,512]{1,0:T(8,128)S(1)}, f32[32,256,512]{2,1,0:T(8,128)}, f32[256,1]{0,1:T(1,128)S(1)}, /*in...) while((s32[]{:T(128)}, f32[256,512]{1,0:T(8,128)S(1)}, f32[32,512]{1,0:T(8,128)S(1)}, ...), condition=%wide.region_11.13_spmd, body=%wide.region_9.12_spmd.sunk | while | flops 916995 | bytes 1586301 | solution.py:55
  761.3 7.6 gather_fusion.24
  771.7 13.1 %all-to-all-start.13 = ((f32[128,1,512]{2,1,0:T(1,128)}), f32[128,1,512]{2,1,0:T(1,128)S(1)}, u32[]{:S(2)}, u32[]{:S(2)}) async-start(f32[128,1,512]{2,1,0:T(1,128)} %reshape.736), calls=%async_computation.13 | async-start | bytes 524288 | tf_op jit(solution)/shard_map/all_to_all | solution.py:229
  786.0 10.3 %all-to-all-done.13 = f32[128,1,512]{2,1,0:T(1,128)S(1)} async-done(((f32[128,1,512]{2,1,0:T(1,128)}), f32[128,1,512]{2,1,0:T(1,128)S(1)}, u32[]{:S(2)}, u32[]{:S(2)}) %all-to-all-start.13) | async-done | bytes 262176 | tf_op jit(solution)/shard_map/all_to_all | solution.py:229
  801.8 10.0 %all-to-all-done.4 = f32[128,1,512]{2,1,0:T(1,128)S(1)} async-done(((f32[128,1,512]{2,1,0:T(1,128)}), f32[128,1,512]{2,1,0:T(1,128)S(1)}, u32[]{:S(2)}, u32[]{:S(2)}) %all-to-all-start.4) | async-done | bytes 262176 | tf_op jit(solution)/shard_map/all_to_all | solution.py:228
  (1265 shorter events, 672.7 us)
Async XLA Ops:
  0.6 10.6 %copy-start = (f32[1024]{0:T(1024)S(1)}, f32[1024]{0:T(1024)}, u32[]{:S(2)}) copy-start(f32[1024]{0:T(1024)} %param.45) | copy-start | bytes 12292
  16.4 18.4 %copy-start.14 = (pred[1024]{0:T(1024)(128)(4,1)}, pred[1024]{0:T(1024)(128)(4,1)S(1)}, u32[]{:S(2)}) copy-start(pred[1024]{0:T(1024)(128)(4,1)S(1)} %get-tuple-element.809) | copy-start | bytes 3076
  16.4 13.9 %copy-start.2 = (f32[1024]{0:T(1024)S(1)}, f32[1024]{0:T(1024)}, u32[]{:S(2)}) copy-start(f32[1024]{0:T(1024)} %param.44) | copy-start | bytes 12292
  21.6 73.7 %all-to-all-start.5 = ((f32[1,16,64]{2,0,1:T(1,128)}), f32[1,16,64]{2,0,1:T(1,128)S(1)}, u32[]{:S(2)}, u32[]{:S(2)}) async-start(f32[1,16,64]{2,0,1:T(1,128)} %reshape.630), calls=%async_computation.5 | async-start | bytes 16384 | tf_op jit(solution)/shard_map/all_to_all | solution.py:199
  95.3 12.9 %all-to-all-start.6 = ((f32[1,16,64]{2,0,1:T(1,128)}), f32[1,16,64]{2,0,1:T(1,128)S(1)}, u32[]{:S(2)}, u32[]{:S(2)}) async-start(f32[1,16,64]{2,0,1:T(1,128)} %reshape.627), calls=%async_computation.6 | async-start | bytes 16384 | tf_op jit(solution)/shard_map/all_to_all | solution.py:182
  108.2 11.8 %all-to-all-start.11 = ((f32[1,16,64]{2,0,1:T(1,128)}), f32[1,16,64]{2,0,1:T(1,128)S(1)}, u32[]{:S(2)}, u32[]{:S(2)}) async-start(f32[1,16,64]{2,0,1:T(1,128)} %reshape.629), calls=%async_computation.11 | async-start | bytes 16384 | tf_op jit(solution)/shard_map/all_to_all | solution.py:189
  120.0 18.1 %all-to-all-start.1 = ((f32[1,128,16]{2,0,1:T(1,128)}), f32[1,128,16]{2,0,1:T(1,128)S(1)}, u32[]{:S(2)}, u32[]{:S(2)}) async-start(f32[1,128,16]{2,0,1:T(1,128)} %bitcast.29), calls=%async_computation.1 | async-start | bytes 131072 | tf_op jit(solution)/shard_map/all_to_all | solution.py:150
  132.0 14.6 %copy-start.33 = (f32[224]{0:T(256)S(1)}, f32[224]{0:T(256)}, u32[]{:S(2)}) copy-start(f32[224]{0:T(256)} %param.49) | copy-start | bytes 2692
  138.1 15.7 %all-to-all-start.3 = ((f32[128,1,512]{2,1,0:T(1,128)}), f32[128,1,512]{2,1,0:T(1,128)S(1)}, u32[]{:S(2)}, u32[]{:S(2)}) async-start(f32[128,1,512]{2,1,0:T(1,128)} %reshape.724), calls=%async_computation.3 | async-start | bytes 524288 | tf_op jit(solution)/shard_map/all_to_all | solution.py:147
  142.4 26.8 %copy-start.25 = (f32[512]{0:T(512)}, f32[512]{0:T(512)S(1)}, u32[]{:S(2)}) copy-start(f32[512]{0:T(512)S(1)} %get-tuple-element.1288) | copy-start | bytes 6148
  142.4 108.7 %copy-start.26 = (pred[512]{0:T(512)(128)(4,1)}, pred[512]{0:T(512)(128)(4,1)S(1)}, u32[]{:S(2)}) copy-start(pred[512]{0:T(512)(128)(4,1)S(1)} %get-tuple-element.811) | copy-start | bytes 1540
  153.8 15.4 %all-to-all-start.2 = ((f32[128,1,512]{2,1,0:T(1,128)}), f32[128,1,512]{2,1,0:T(1,128)S(1)}, u32[]{:S(2)}, u32[]{:S(2)}) async-start(f32[128,1,512]{2,1,0:T(1,128)} %reshape.722), calls=%async_computation.2 | async-start | bytes 524288 | tf_op jit(solution)/shard_map/all_to_all | solution.py:149
  169.2 18.1 %all-to-all-start = ((f32[128,1,512]{2,1,0:T(1,128)}), f32[128,1,512]{2,1,0:T(1,128)S(1)}, u32[]{:S(2)}, u32[]{:S(2)}) async-start(f32[128,1,512]{2,1,0:T(1,128)} %reshape.720), calls=%async_computation | async-start | bytes 524288 | tf_op jit(solution)/shard_map/all_to_all | solution.py:148
  187.4 12.8 %copy-start.6 = (f32[1024,32]{1,0:T(8,128)S(1)}, f32[1024,32]{1,0:T(8,128)}, u32[]{:S(2)}) copy-start(f32[1024,32]{1,0:T(8,128)} %gather_fusion.12) | copy-start | bytes 393220
  187.4 26.9 %all-to-all-start.9 = ((bf16[128,16,64]{0,2,1:T(8,128)(2,1)}), bf16[128,16,64]{0,2,1:T(8,128)(2,1)S(1)}, u32[]{:S(2)}, u32[]{:S(2)}) async-start(bf16[128,16,64]{0,2,1:T(8,128)(2,1)} %broadcast_select_fusion.11), calls=%async_computation.9 | async-start | bytes 524288 | tf_op jit(solution)/shard_map/all_to_all | solution.py:202
  214.2 13.6 %all-to-all-start.10 = ((f32[16,1,2048]{2,1,0:T(1,128)}), f32[16,1,2048]{2,1,0:T(1,128)}, u32[]{:S(2)}, u32[]{:S(2)}) async-start(f32[16,1,2048]{2,1,0:T(1,128)} %reshape.732), calls=%async_computation.10 | async-start | bytes 262144 | tf_op jit(solution)/shard_map/all_to_all | solution.py:179
  227.8 10.3 %all-to-all-start.7 = ((f32[16,1,2048]{2,1,0:T(1,128)}), f32[16,1,2048]{2,1,0:T(1,128)S(1)}, u32[]{:S(2)}, u32[]{:S(2)}) async-start(f32[16,1,2048]{2,1,0:T(1,128)} %reshape.728), calls=%async_computation.7 | async-start | bytes 262144 | tf_op jit(solution)/shard_map/all_to_all | solution.py:176
  238.2 10.7 %all-to-all-start.8 = ((f32[16,1,2048]{2,1,0:T(1,128)}), f32[16,1,2048]{2,1,0:T(1,128)S(1)}, u32[]{:S(2)}, u32[]{:S(2)}) async-start(f32[16,1,2048]{2,1,0:T(1,128)} %reshape.730), calls=%async_computation.8 | async-start | bytes 262144 | tf_op jit(solution)/shard_map/all_to_all | solution.py:196
  251.6 102.1 %copy-start.27 = (pred[512]{0:T(512)(128)(4,1)S(1)}, pred[512]{0:T(512)(128)(4,1)}, u32[]{:S(2)}) copy-start(pred[512]{0:T(512)(128)(4,1)} %copy-done.26) | copy-start | bytes 1540
  251.7 102.1 %copy-start.28 = (f32[512]{0:T(512)S(1)}, f32[512]{0:T(512)}, u32[]{:S(2)}) copy-start(f32[512]{0:T(512)} %gather_fusion.22) | copy-start | bytes 6148
  401.9 355.2 %all-to-all-start.12 = ((f32[16,1,2048]{2,1,0:T(1,128)}), f32[16,1,2048]{2,1,0:T(1,128)S(1)}, u32[]{:S(2)}, u32[]{:S(2)}) async-start(f32[16,1,2048]{2,1,0:T(1,128)} %reshape.734), calls=%async_computation.12 | async-start | bytes 262144 | tf_op jit(solution)/shard_map/all_to_all | solution.py:221
  770.6 29.7 %copy-start.20 = (s32[1024]{0:T(1024)S(1)}, s32[1024]{0:T(1024)}, u32[]{:S(2)}) copy-start(s32[1024]{0:T(1024)} %copy-done.19) | copy-start | bytes 12292
  771.7 24.6 %all-to-all-start.13 = ((f32[128,1,512]{2,1,0:T(1,128)}), f32[128,1,512]{2,1,0:T(1,128)S(1)}, u32[]{:S(2)}, u32[]{:S(2)}) async-start(f32[128,1,512]{2,1,0:T(1,128)} %reshape.736), calls=%async_computation.13 | async-start | bytes 524288 | tf_op jit(solution)/shard_map/all_to_all | solution.py:229
  796.3 15.5 %all-to-all-start.4 = ((f32[128,1,512]{2,1,0:T(1,128)}), f32[128,1,512]{2,1,0:T(1,128)S(1)}, u32[]{:S(2)}, u32[]{:S(2)}) async-start(f32[128,1,512]{2,1,0:T(1,128)} %reshape.726), calls=%async_computation.4 | async-start | bytes 524288 | tf_op jit(solution)/shard_map/all_to_all | solution.py:228
  (25 other events, 156.2 us)
where the time goes:
time: 830 us; the launch traced here: 821 us
  matrix products  257 us (31%)
  local copies, waits for them, and re-layouts  226 us (27%)
  other arithmetic  187 us (23%)
  starting transfers between devices  88.6 us (11%)
  waiting for transfers between devices  52.2 us (6%)
  loops' own time  8.56 us (1%)
    dot_general x96, matrix products, optical_depth(): jnp.dot(table, corner_weights(index_row, weight_rows), preferred_element_...  257 us
    reduce_sum x64, other arithmetic, longwave_upward(): return (flux_out, jnp.sum(flux_in - flux_out, axis=0))  81.8 us
    gather x16, local copies, waits for them, and re-layouts, gather_cols(): return jnp.take(values, index, axis=-1, mode='fill', fill_value=blank)  78.9 us
    dynamic_update_slice x256, local copies, waits for them, and re-layouts, longwave(): lax.scan(longwave_downward, initial, (index_cols, weight_levels, path_col...  62.7 us
    reduce_sum x32, other arithmetic, shortwave_upward(): return (flux_out, jnp.sum(flux_in - flux_out, axis=0))  40.9 us
    dynamic_update_slice x32, other arithmetic, shortwave(): lax.scan(shortwave_downward, initial, (index_cols, weight_levels, path_co...  27.3 us
  transfers between devices with their start and end apart: 14, of which 9 were waited for; matrix products, arithmetic and copies ran while one was open for 58% of the time, Pallas kernels for 0%

commit v1 on v0

v1 whole, which is shorter than its diff:
```python
from functools import partial

import jax
import jax.numpy as jnp
from jax import lax
from jax.experimental import pallas as pl
from jax.experimental.pallas import tpu as pltpu
from jax.sharding import PartitionSpec as P

F32, BF16, I32, I16 = jnp.float32, jnp.bfloat16, jnp.int32, jnp.int16
TEMPS, PRESS, LEV = 14, 64, 32
NTAB = TEMPS * PRESS
KPAD = 1024
CAP = 16
SW_CAP = 64
LOG2E = 1.4426950408889634
DIFF = -1.66 * LOG2E
CODES = ((0.5, 1.0), (0.2, 2.8), (0.0, 0.6))
BLOCK = 256
VMEM_LIMIT = 60 * 1024 * 1024
NT = (((1,), (1,)), ((), ()))
TN = (((0,), (0,)), ((), ()))


def iota(shape, axis, dtype=I32):
    return lax.broadcasted_iota(dtype, shape, axis)


def one_hot(left, right):
    return jnp.where(left == right, 1.0, 0.0).astype(BF16)


def split3(x):
    a = x.astype(BF16)
    rest = x - a.astype(F32)
    b = rest.astype(BF16)
    c = (rest - b.astype(F32)).astype(BF16)
    return a, b, c


def dealt_rank(mark):
    parties, columns = mark.shape
    below = one_hot_less()
    before = jnp.zeros((parties, 1), F32)
    ranks = []
    for k in range(columns // 128):
        part = mark[:, k * 128 : (k + 1) * 128]
        running = jnp.dot(part.astype(BF16), below, preferred_element_type=F32) + before
        ranks.append(jnp.sum(running * part, axis=0, keepdims=True))
        before = before + jnp.sum(part, axis=1, keepdims=True)
    return jnp.concatenate(ranks, axis=1)


def one_hot_less():
    return jnp.where(iota((128, 128), 0) < iota((128, 128), 1), 1.0, 0.0).astype(BF16)


def pack_kernel(planck_ref, path_ref, cloud_ref, map_ref, send_ref, slot_ref):
    columns = map_ref.shape[1]
    devices = send_ref.shape[0] // CAP
    span = map_ref[...]
    shift = columns.bit_length() - 1
    target = lax.shift_right_logical(span, shift)
    mark = jnp.where(iota((devices, columns), 0) == target, 1.0, 0.0)
    slot = target * CAP + dealt_rank(mark).astype(I32)
    slot_ref[...] = slot
    codes = []
    for ref, (low, width) in zip((planck_ref, path_ref, cloud_ref), CODES):
        scaled = (ref[...] - low) * (65535.0 / width) + 0.5
        codes.append(jnp.clip(scaled, 0.0, 65535.0).astype(I32))
    codes.append(jnp.broadcast_to(span & (columns - 1), (LEV, columns)))
    code = jnp.concatenate(codes, axis=0)
    high = lax.shift_right_logical(code, 8).astype(F32).astype(BF16)
    low = (code & 255).astype(F32).astype(BF16)
    both = jnp.concatenate([high, low], axis=0)
    rows = 512
    for k in range(send_ref.shape[0] // rows):
        pick = one_hot(iota((rows, columns), 0) + k * rows, slot)
        got = lax.dot_general(pick, both, NT, preferred_element_type=F32)
        width = 4 * LEV
        value = got[:, :width] * 256.0 + got[:, width:] - 32768.0
        send_ref[pl.ds(k * rows, rows), :] = value.astype(I32).astype(I16)


def radiation_kernel(
    recv_ref,
    surface_ref,
    index_ref,
    weight_ref,
    sunlit_ref,
    slot_ref,
    cosine_ref,
    albedo_ref,
    table_lw_ref,
    table_sw_ref,
    frac_ref,
    solar_ref,
    back_ref,
    ground_ref,
    phys,
    weights,
    planck_ext,
    ratio,
    table,
    mixing,
    absorb,
    transmit,
    state_lw,
    state_sw,
    frac_col,
    solar_col,
    heat,
    gain,
):
    columns = index_ref.shape[1]
    slots = recv_ref.shape[0]
    g_lw, g_sw = table_lw_ref.shape[0], table_sw_ref.shape[0]
    g_all = g_lw + g_sw
    code = recv_ref[...].astype(I32) + 32768
    both = jnp.concatenate(
        [lax.shift_right_logical(code, 8).astype(F32).astype(BF16), (code & 255).astype(F32).astype(BF16)], axis=1
    )
    label = code[:, 3 * LEV : 3 * LEV + 1] - 0
    for k in range(columns // BLOCK):
        pick = one_hot(label, iota((slots, BLOCK), 1) + k * BLOCK)
        got = lax.dot_general(both, pick, TN, preferred_element_type=F32)
        value = got[: 4 * LEV] * 256.0 + got[4 * LEV :]
        for n, (low, width) in enumerate(CODES):
            phys[pl.ds(n * LEV, LEV), pl.ds(k * BLOCK, BLOCK)] = value[n * LEV : (n + 1) * LEV] * (width / 65535.0) + low
    planck = phys[0:LEV, :]
    path = phys[LEV : 2 * LEV, :]
    cloud = phys[2 * LEV : 3 * LEV, :]
    planck_ext[0:1, :] = jnp.zeros((1, columns), F32)
    planck_ext[pl.ds(1, LEV), :] = planck
    planck_ext[pl.ds(LEV + 1, 1), :] = surface_ref[...]
    ratio[...] = cloud / path
    for k in range(4):
        weights[pl.ds(k * LEV, LEV), :] = weight_ref[k].astype(F32)
    ones = jnp.where(iota((g_all, 128), 1) < 3, 1.0, 0.0).astype(BF16)
    table[:g_lw, :NTAB] = table_lw_ref[...]
    table[g_lw:, :NTAB] = table_sw_ref[...]
    table[:, NTAB:] = ones
    mixing[NTAB:, :] = jnp.zeros((KPAD - NTAB, BLOCK), BF16)
    frac = jnp.sum(jnp.where(iota((g_lw, g_lw), 0) == iota((g_lw, g_lw), 1), frac_ref[...], 0.0), axis=1, keepdims=True)
    solar = jnp.sum(jnp.where(iota((g_sw, g_sw), 0) == iota((g_sw, g_sw), 1), solar_ref[...], 0.0), axis=1, keepdims=True)
    frac_col[...] = jnp.broadcast_to(frac, frac_col.shape)
    solar_col[...] = jnp.broadcast_to(solar, solar_col.shape)
    total = jnp.sum(frac_ref[...])
    rows = 32

    def one_block(k, _):
        base = pl.multiple_of(k * BLOCK, BLOCK)
        here = pl.ds(base, BLOCK)
        state_lw[...] = jnp.zeros_like(state_lw)
        cosine = cosine_ref[:, here]
        inverse = -LOG2E / cosine
        top_beam = jnp.zeros((8, BLOCK), F32)
        for r in range(0, g_sw, 8):
            beam = solar_col[r : r + 8, :] * cosine
            state_sw[r : r + 8, :] = beam
            top_beam = top_beam + beam

        def downward(level, before):
            flux_before, beam_before = before
            row = pl.ds(level, 1)
            index = index_ref[row, here]
            temp = lax.shift_right_logical(index, 6).astype(F32).astype(BF16)
            press = index & 63
            w = [weights[pl.ds(c * LEV + level, 1), here] for c in range(4)]
            p_of = iota((PRESS, BLOCK), 0)
            at0, at1 = p_of == press, p_of == press + 1
            low = jnp.where(at0, w[0], jnp.where(at1, w[1], 0.0)).astype(BF16)
            wrap = (p_of == 0) & (press == PRESS - 1)
            high = jnp.where(at0, w[2], jnp.where(at1, w[3], jnp.where(wrap, w[1], 0.0))).astype(BF16)
            over = jnp.where(wrap, w[3], 0.0)[:16].astype(BF16)
            temps = jnp.broadcast_to(temp, (16, BLOCK))
            zero = jnp.zeros((16, BLOCK), BF16)
            is_temp = [temps == jnp.asarray(t, BF16) for t in range(TEMPS)]
            for t in range(TEMPS):
                for p in range(0, PRESS, 16):
                    tile = zero
                    if p == 0 and t >= 2:
                        tile = jnp.where(is_temp[t - 2], over, tile)
                    if t >= 1:
                        tile = jnp.where(is_temp[t - 1], high[p : p + 16], tile)
                    tile = jnp.where(is_temp[t], low[p : p + 16], tile)
                    mixing[t * PRESS + p : t * PRESS + p + 16, :] = tile
            pieces = split3(ratio[row, here])
            tail = [jnp.broadcast_to(x.astype(F32), (16, BLOCK)) for x in pieces]
            which = iota((16, BLOCK), 0)
            mixing[NTAB : NTAB + 16, :] = jnp.where(
                which == 0, tail[0], jnp.where(which == 1, tail[1], jnp.where(which == 2, tail[2], 0.0))
            ).astype(BF16)
            absorb[...] = jnp.dot(table[...], mixing[...], preferred_element_type=F32)
            path_row = phys[pl.ds(LEV + level, 1), here]
            diffuse = path_row * DIFF
            direct = path_row * inverse
            step = planck_ext[pl.ds(level, 1), here] - planck_ext[pl.ds(level + 1, 1), here]
            acc = jnp.zeros((8, BLOCK), F32)
            for r in range(0, g_lw, 8):
                t = jnp.exp2(absorb[r : r + 8, :] * diffuse)
                transmit[level, r : r + 8, :] = t
                e = t * (state_lw[r : r + 8, :] + step)
                state_lw[r : r + 8, :] = e
                acc = acc + e * frac_col[r : r + 8, :]
            acc_sw = jnp.zeros((8, BLOCK), F32)
            for r in range(0, g_sw, 8):
                a = absorb[g_lw + r : g_lw + r + 8, :]
                transmit[level, g_lw + r : g_lw + r + 8, :] = jnp.exp2(a * diffuse)
                b = state_sw[r : r + 8, :] * jnp.exp2(a * direct)
                state_sw[r : r + 8, :] = b
                acc_sw = acc_sw + b
            flux = jnp.sum(acc, axis=0, keepdims=True) + planck_ext[pl.ds(level + 1, 1), here] * total
            beam = jnp.sum(acc_sw, axis=0, keepdims=True)
            heat[row, here] = flux_before - flux
            heat[pl.ds(LEV + level, 1), here] = beam_before - beam
            return flux, beam

        start = (jnp.zeros((1, BLOCK), F32), jnp.sum(top_beam, axis=0, keepdims=True))
        _, ground_beam = lax.fori_loop(0, LEV, downward, start)
        albedo = albedo_ref[:, here]
        gain[0:1, here] = (1.0 - albedo) * ground_beam
        state_lw[...] = jnp.zeros_like(state_lw)
        for r in range(0, g_sw, 8):
            state_sw[r : r + 8, :] = state_sw[r : r + 8, :] * albedo

        def upward(n, before):
            level = LEV - 1 - n
            flux_before, up_before = before
            row = pl.ds(level, 1)
            own = planck_ext[pl.ds(level + 1, 1), here]
            step = planck_ext[pl.ds(level + 2, 1), here] - own
            acc = jnp.zeros((8, BLOCK), F32)
            for r in range(0, g_lw, 8):
                e = transmit[level, r : r + 8, :] * (state_lw[r : r + 8, :] + step)
                state_lw[r : r + 8, :] = e
                acc = acc + e * frac_col[r : r + 8, :]
            acc_sw = jnp.zeros((8, BLOCK), F32)
            for r in range(0, g_sw, 8):
                v = transmit[level, g_lw + r : g_lw + r + 8, :] * state_sw[r : r + 8, :]
                state_sw[r : r + 8, :] = v
                acc_sw = acc_sw + v
            flux = jnp.sum(acc, axis=0, keepdims=True) + own * total
            up = jnp.sum(acc_sw, axis=0, keepdims=True)
            heat[row, here] = heat[row, here] + (flux_before - flux)
            heat[pl.ds(LEV + level, 1), here] = heat[pl.ds(LEV + level, 1), here] + (up_before - up)
            return flux, up

        lax.fori_loop(0, LEV, upward, (surface_ref[:, here] * total, ground_beam * albedo))
        return 0

    lax.fori_loop(0, columns // BLOCK, one_block, 0)

    sunlit = sunlit_ref[...]
    result = jnp.concatenate([heat[0:LEV, :], heat[LEV:, :] * sunlit.astype(F32)], axis=0)
    first = result.astype(BF16)
    second = (result - first.astype(F32)).astype(BF16)
    both = jnp.concatenate([first, second], axis=0)
    rows = 512
    for k in range(slots // rows):
        part = recv_ref[pl.ds(k * rows, rows), :].astype(I32) + 32768
        pick = one_hot(part[:, 3 * LEV : 3 * LEV + 1], iota((rows, columns), 1))
        back_ref[pl.ds(k * rows, rows), :] = lax.dot_general(pick, both, NT, preferred_element_type=F32).astype(BF16)

    owners = ground_ref.shape[0]
    sw_count = columns // 2
    sw_slot = slot_ref[...]
    owner = jnp.where(sunlit == 1, lax.shift_right_logical(sw_slot, sw_count.bit_length() - 1), owners)
    mark = jnp.where(iota((owners, columns), 0) == owner, 1.0, 0.0)
    place = owner * 128 + dealt_rank(mark).astype(I32)
    a, b, c = split3(gain[0:1, :])
    own_slot = sw_slot & (sw_count - 1)
    label_high = lax.shift_right_logical(own_slot, 5).astype(F32) + 1.0
    label_low = (own_slot & 31).astype(F32)
    stack = jnp.zeros((16, columns), F32)
    at = iota((16, columns), 0)
    for n, x in enumerate((a.astype(F32), b.astype(F32), c.astype(F32), label_high, label_low)):
        stack = jnp.where(at == n, x, stack)
    stack = stack.astype(BF16)
    for o in range(owners):
        pick = one_hot(iota((128, columns), 0) + o * 128, place)
        got = lax.dot_general(stack, pick, NT, preferred_element_type=F32)
        value = got[0:1] + got[1:2] + got[2:3]
        label = got[3:4] * 32.0 + got[4:5] - 32.0
        ground_ref[o] = jnp.where(iota((8, 128), 0) == 0, value, label)


def home_kernel(back_ref, slot_ref, lw_ref, sw_ref):
    columns = slot_ref.shape[1]
    slots = back_ref.shape[0]
    got = jnp.zeros((4 * LEV, columns), F32)
    rows = 512
    for k in range(slots // rows):
        pick = one_hot(iota((rows, columns), 0) + k * rows, slot_ref[...])
        got = got + lax.dot_general(back_ref[pl.ds(k * rows, rows), :], pick, TN, preferred_element_type=F32)
    value = got[: 2 * LEV] + got[2 * LEV :]
    lw_ref[...] = value[:LEV]
    sw_ref[...] = value[LEV:]


def surface_kernel(ground_ref, out_ref):
    count = out_ref.shape[1]
    total = jnp.zeros((16, count), F32)
    for o in range(ground_ref.shape[0]):
        got = ground_ref[o]
        pick = one_hot(got[1:2].astype(I32), iota((count, 128), 0))
        a, b, c = split3(got[0:1])
        at = iota((16, 128), 0)
        stack = jnp.where(at == 0, a.astype(F32), jnp.where(at == 1, b.astype(F32), jnp.where(at == 2, c.astype(F32), 0.0)))
        total = total + lax.dot_general(stack.astype(BF16), pick, NT, preferred_element_type=F32)
    out_ref[...] = total[0:1] + total[1:2] + total[2:3]


def params():
    return pltpu.CompilerParams(vmem_limit_bytes=VMEM_LIMIT)


def vmem(count):
    return [pl.BlockSpec(memory_space=pltpu.VMEM)] * count


def body(
    planck_source,
    absorber_path,
    cloud_depth,
    span_map,
    surface_source,
    interp_index,
    interp_weight,
    sunlit,
    sw_slot,
    cos_zenith,
    albedo,
    table_lw,
    table_sw,
    planck_frac,
    solar_weight,
):
    columns = span_map.shape[0]
    owners = lax.axis_size("col")
    devices = lax.axis_size("dyn") * owners
    slots = devices * CAP
    g_lw, g_sw = table_lw.shape[0], table_sw.shape[0]

    def row(x):
        return x.reshape(1, -1)

    send, slot = pl.pallas_call(
        pack_kernel,
        out_shape=(jax.ShapeDtypeStruct((slots, 128), I16), jax.ShapeDtypeStruct((1, columns), I32)),
        in_specs=vmem(4),
        out_specs=tuple(vmem(2)),
        compiler_params=params(),
        name="pack",
    )(planck_source, absorber_path, cloud_depth, row(span_map))
    recv = lax.all_to_all(send.reshape(devices, CAP, 128), ("dyn", "col"), 0, 0, tiled=True)
    back, ground = pl.pallas_call(
        radiation_kernel,
        out_shape=(jax.ShapeDtypeStruct((slots, 128), BF16), jax.ShapeDtypeStruct((owners, 8, 128), F32)),
        in_specs=vmem(12),
        out_specs=tuple(vmem(2)),
        scratch_shapes=[
            pltpu.VMEM((3 * LEV, columns), F32),
            pltpu.VMEM((4 * LEV, columns), F32),
            pltpu.VMEM((40, columns), F32),
            pltpu.VMEM((LEV, columns), F32),
            pltpu.VMEM((g_lw + g_sw, KPAD), BF16),
            pltpu.VMEM((KPAD, BLOCK), BF16),
            pltpu.VMEM((g_lw + g_sw, BLOCK), F32),
            pltpu.VMEM((LEV, g_lw + g_sw, BLOCK), F32),
            pltpu.VMEM((g_lw, BLOCK), F32),
            pltpu.VMEM((g_sw, BLOCK), F32),
            pltpu.VMEM((g_lw, BLOCK), F32),
            pltpu.VMEM((g_sw, BLOCK), F32),
            pltpu.VMEM((2 * LEV, columns), F32),
            pltpu.VMEM((8, columns), F32),
        ],
        compiler_params=params(),
        name="radiation",
    )(
        recv.reshape(slots, 128),
        row(surface_source),
        interp_index,
        interp_weight,
        row(sunlit),
        row(sw_slot),
        row(cos_zenith),
        row(albedo),
        table_lw,
        table_sw,
        row(planck_frac),
        row(solar_weight),
    )
    ground_in = lax.all_to_all(ground, "col", 0, 0, tiled=True)
    home = lax.all_to_all(back.reshape(devices, CAP, 128), ("dyn", "col"), 0, 0, tiled=True)
    surface = pl.pallas_call(
        surface_kernel,
        out_shape=jax.ShapeDtypeStruct((1, columns // 2), F32),
        in_specs=vmem(1),
        out_specs=vmem(1)[0],
        compiler_params=params(),
        name="surface",
    )(ground_in)
    heating_lw, heating_sw = pl.pallas_call(
        home_kernel,
        out_shape=(jax.ShapeDtypeStruct((LEV, columns), F32),) * 2,
        in_specs=vmem(2),
        out_specs=tuple(vmem(2)),
        compiler_params=params(),
        name="home",
    )(home.reshape(slots, 128), slot)
    return (heating_lw, heating_sw, surface.reshape(-1))


def solution(mesh):
    columns = P(None, ("dyn", "col"))
    flat = P(("dyn", "col"))
    in_specs = (
        columns, columns, columns, flat, flat, columns, P(None, None, ("dyn", "col")),
        flat, flat, flat, flat, P(), P(), P(), P(),
    )
    out_specs = (columns, columns, flat)
    return jax.shard_map(body, mesh=mesh, in_specs=in_specs, out_specs=out_specs, check_vma=False)
```

time: 830 us -> 142 us (0.17); the launches traced: 821 us -> 142 us
  matrix products: 257 us -> 0 us
  local copies, waits for them, and re-layouts: 226 us -> 0.79 us
  other arithmetic: 187 us -> 0 us
  Pallas kernels: 0 us -> 86.8 us
  starting transfers between devices: 88.6 us -> 5.21 us
  waiting for transfers between devices: 52.2 us -> 12.1 us
  blocking collectives: 0 us -> 36.3 us
  loops' own time: 8.56 us -> 0 us
    dot_general x96 -> x0, matrix products: 257 us -> none  [optical_depth(): jnp.dot(table, corner_weights(index_row, weight_rows), preferred_element_...]
    reduce_sum x99 -> x0, other arithmetic: 123 us -> none  [the longest x64 81.8 us: longwave_upward(): return (flux_out, jnp.sum(flux_in - flux_out, axis=0))]
    gather x28 -> x0, local copies, waits for them, and re-layouts: 107 us -> none  [the longest x16 78.9 us: gather_cols(): return jnp.take(values, index, axis=-1, mode='fill', fill_value=blank)]
    pallas_call x0 -> x4, Pallas kernels: none -> 86.8 us  [the longest x1 78.8 us: body(): pl.pallas_call(radiation_kernel, out_shape=(jax.ShapeDtypeStruct((slots,...]
    all_to_all x14 -> x1, starting transfers between devices: 88.6 us -> 5.21 us  [body(): lax.all_to_all(back.reshape(devices, CAP, 128), ('dyn', 'col'), 0, 0, til...]
    dynamic_update_slice x256 -> x0, local copies, waits for them, and re-layouts: 62.7 us -> none  [longwave(): lax.scan(longwave_downward, initial, (index_cols, weight_levels, path_col...]
    all_to_all x14 -> x1, waiting for transfers between devices: 52.2 us -> 12.1 us  [body(): lax.all_to_all(back.reshape(devices, CAP, 128), ('dyn', 'col'), 0, 0, til...]
    all_to_all x0 -> x2, blocking collectives: none -> 36.3 us  [the longest x1 25.7 us: body(): lax.all_to_all(send.reshape(devices, CAP, 128), ('dyn', 'col'), 0, 0, til...]
  transfers between devices with their start and end apart: 14 -> 1, of which waited for: 9 -> 1; matrix products, arithmetic and copies ran while one was open for 58% -> 0% of each run, Pallas kernels for 0% -> 1%
where the time goes in v1:
time: 142 us
  Pallas kernels  86.8 us (61%)
  blocking collectives  36.3 us (26%)
  waiting for transfers between devices  12.1 us (9%)
  starting transfers between devices  5.21 us (4%)
    pallas_call x1, Pallas kernels, body(): pl.pallas_call(radiation_kernel, out_shape=(jax.ShapeDtypeStruct((slots,...  78.8 us
    all_to_all x1, blocking collectives, body(): lax.all_to_all(send.reshape(devices, CAP, 128), ('dyn', 'col'), 0, 0, til...  25.7 us
    all_to_all x1, waiting for transfers between devices, body(): lax.all_to_all(back.reshape(devices, CAP, 128), ('dyn', 'col'), 0, 0, til...  12.1 us
    all_to_all x1, blocking collectives, body(): ground_in = lax.all_to_all(ground, 'col', 0, 0, tiled=True)  10.6 us
    all_to_all x1, starting transfers between devices, body(): lax.all_to_all(back.reshape(devices, CAP, 128), ('dyn', 'col'), 0, 0, til...  5.21 us
    pallas_call x1, Pallas kernels, body(): pl.pallas_call(pack_kernel, out_shape=(jax.ShapeDtypeStruct((slots, 128),...  3.34 us
  transfers between devices with their start and end apart: 1, of which 1 were waited for; matrix products, arithmetic and copies ran while one was open for 0% of the time, Pallas kernels for 1%

profile of v1, /device:TPU:1, one launch (start us, length us, event | category | flops | bytes accessed | tf_op | source)
XLA Modules:
  0.0 141.8 jit_solution(790875613688816077)
XLA Ops:
  0.6 3.3 %pack.1 = (s16[2048,128]{1,0:T(8,128)(2,1)}, s32[1,1024]{1,0:T(1,128)}) custom-call(f32[32,1024]{1,0:T(8,128)} %planck_ref.1, f32[32,1024]{1,0:T(8,128)} %path_ref.1, f32[32,1024]{1,0:T(8,128)} %cloud_ref.1, s32[1,1024]{1,0:T(1,128)} %bitcast.17), custom_call_target="tpu_custom_call" | custom-call | tf_op jit(solution)/shard_map/pack/pallas_call | solution.py:348
  4.0 25.7 %all_to_all.15 = s16[128,16,128]{2,1,0:T(8,128)(2,1)} all-to-all(s16[128,16,128]{2,1,0:T(8,128)(2,1)} %bitcast.16), channel_id=1, replica_groups=mesh['dyn'=8,'col'=16] {'dyn','col'}, dimensions={0} | all-to-all | bytes 1048576 | tf_op jit(solution)/shard_map/all_to_all | solution.py:356
  29.7 78.8 %radiation.1 = (bf16[2048,128]{1,0:T(8,128)(2,1)}, f32[16,8,128]{2,1,0:T(8,128)}) custom-call(s16[2048,128]{1,0:T(8,128)(2,1)} %bitcast.14, f32[1,1024]{1,0:T(1,128)} %bitcast.18, s32[32,1024]{1,0:T(8,128)} %index_ref.1, bf16[4,32,1024]{2,1,0:T(8,128)(2,1)} %weight_ref.1, s32[1,1024]{1,0:T(1,128)} %bitcast.19, s32[1,1024]{1,0:T(1,128)} %bitcast.20, ...), custom_call_target="tpu_custom_call" | custom-call | tf_op jit(solution)/shard_map/radiation/pallas_call | solution.py:357
  108.5 10.6 %all_to_all.16.ground_ref = f32[16,8,128]{2,1,0:T(8,128)} all-to-all(f32[16,8,128]{2,1,0:T(8,128)} %get-tuple-element.14), channel_id=1, replica_groups=mesh['dyn'=8,'col'=16] {'col'}, dimensions={0} | all-to-all | bytes 131072 | tf_op jit(solution)/shard_map/all_to_all | solution.py:394
  119.1 5.2 %all-to-all-start.1 = ((bf16[128,16,128]{2,1,0:T(8,128)(2,1)}), bf16[128,16,128]{2,1,0:T(8,128)(2,1)S(1)}, u32[]{:S(2)}, u32[]{:S(2)}) async-start(bf16[128,16,128]{2,1,0:T(8,128)(2,1)} %bitcast.15), calls=%async_computation.1 | async-start | bytes 1048576 | tf_op jit(solution)/shard_map/all_to_all | solution.py:395
  124.3 2.1 %surface.1 = f32[1,512]{1,0:T(1,128)} custom-call(f32[16,8,128]{2,1,0:T(8,128)} %all_to_all.16.ground_ref), custom_call_target="tpu_custom_call" | custom-call | tf_op jit(solution)/shard_map/surface/pallas_call | solution.py:396
  126.4 12.1 %all-to-all-done.1 = bf16[128,16,128]{2,1,0:T(8,128)(2,1)S(1)} async-done(((bf16[128,16,128]{2,1,0:T(8,128)(2,1)}), bf16[128,16,128]{2,1,0:T(8,128)(2,1)S(1)}, u32[]{:S(2)}, u32[]{:S(2)}) %all-to-all-start.1) | async-done | bytes 524320 | tf_op jit(solution)/shard_map/all_to_all | solution.py:395
  138.5 0.0 copy-start
  138.5 0.8 copy-done
  139.2 2.6 %home.1 = (f32[32,1024]{1,0:T(8,128)}, f32[32,1024]{1,0:T(8,128)}) custom-call(bf16[2048,128]{1,0:T(8,128)(2,1)} %bitcast.13, s32[1,1024]{1,0:T(1,128)} %get-tuple-element.11.slot_ref), custom_call_target="tpu_custom_call" | custom-call | tf_op jit(solution)/shard_map/home/pallas_call | solution.py:404
Async XLA Ops:
  119.1 19.4 %all-to-all-start.1 = ((bf16[128,16,128]{2,1,0:T(8,128)(2,1)}), bf16[128,16,128]{2,1,0:T(8,128)(2,1)S(1)}, u32[]{:S(2)}, u32[]{:S(2)}) async-start(bf16[128,16,128]{2,1,0:T(8,128)(2,1)} %bitcast.15), calls=%async_computation.1 | async-start | bytes 1048576 | tf_op jit(solution)/shard_map/all_to_all | solution.py:395
  138.5 0.8 copy-start

commit v2 on v1

v2 whole, which is shorter than its diff:
```python
from functools import partial

import jax
import jax.numpy as jnp
from jax import lax
from jax.experimental import pallas as pl
from jax.experimental.pallas import tpu as pltpu
from jax.sharding import PartitionSpec as P

F32, BF16, I32, I16 = jnp.float32, jnp.bfloat16, jnp.int32, jnp.int16
TEMPS, PRESS, LEV = 14, 64, 32
NTAB = TEMPS * PRESS
KPAD = 1024
CAP = 16
SW_CAP = 64
LOG2E = 1.4426950408889634
DIFF = -1.66 * LOG2E
GAIN_SCALE = 8.0
CODES = ((0.5, 1.0), (0.2, 2.8), (0.0, 0.6))
BLOCK = 256
GROUP = 4
VMEM_LIMIT = 60 * 1024 * 1024
NT = (((1,), (1,)), ((), ()))
TN = (((0,), (0,)), ((), ()))


def iota(shape, axis, dtype=I32):
    return lax.broadcasted_iota(dtype, shape, axis)


def one_hot(left, right):
    return jnp.where(left == right, 1.0, 0.0).astype(BF16)


def split3(x):
    a = x.astype(BF16)
    rest = x - a.astype(F32)
    b = rest.astype(BF16)
    c = (rest - b.astype(F32)).astype(BF16)
    return a, b, c


def dealt_rank(mark):
    parties, columns = mark.shape
    below = one_hot_less()
    before = jnp.zeros((parties, 1), F32)
    ranks = []
    for k in range(columns // 128):
        part = mark[:, k * 128 : (k + 1) * 128]
        running = jnp.dot(part.astype(BF16), below, preferred_element_type=F32) + before
        ranks.append(jnp.sum(running * part, axis=0, keepdims=True))
        before = before + jnp.sum(part, axis=1, keepdims=True)
    return jnp.concatenate(ranks, axis=1)


def one_hot_less():
    return jnp.where(iota((128, 128), 0) < iota((128, 128), 1), 1.0, 0.0).astype(BF16)


def pack_kernel(planck_ref, path_ref, cloud_ref, map_ref, send_ref, slot_ref):
    columns = map_ref.shape[1]
    devices = send_ref.shape[0] // CAP
    span = map_ref[...]
    shift = columns.bit_length() - 1
    target = lax.shift_right_logical(span, shift)
    mark = jnp.where(iota((devices, columns), 0) == target, 1.0, 0.0)
    slot = target * CAP + dealt_rank(mark).astype(I32)
    slot_ref[...] = slot
    codes = []
    for ref, (low, width) in zip((planck_ref, path_ref, cloud_ref), CODES):
        scaled = (ref[...] - low) * (65535.0 / width) + 0.5
        codes.append(jnp.clip(scaled, 0.0, 65535.0).astype(I32))
    codes.append(jnp.broadcast_to(span & (columns - 1), (LEV, columns)))
    code = jnp.concatenate(codes, axis=0)
    high = lax.shift_right_logical(code, 8).astype(F32).astype(BF16)
    low = (code & 255).astype(F32).astype(BF16)
    both = jnp.concatenate([high, low], axis=0)
    rows = 512
    for k in range(send_ref.shape[0] // rows):
        pick = one_hot(iota((rows, columns), 0) + k * rows, slot)
        got = lax.dot_general(pick, both, NT, preferred_element_type=F32)
        width = 4 * LEV
        value = got[:, :width] * 256.0 + got[:, width:] - 32768.0
        send_ref[pl.ds(k * rows, rows), :] = value.astype(I32).astype(I16)


def radiation_kernel(
    owners,
    recv_ref,
    surface_ref,
    index_ref,
    weight_ref,
    sunlit_ref,
    slot_ref,
    cosine_ref,
    albedo_ref,
    table_lw_ref,
    table_sw_ref,
    frac_ref,
    solar_ref,
    back_ref,
    phys,
    weights,
    planck_ext,
    ratio,
    table,
    mix_a,
    mix_b,
    out_a,
    out_b,
    transmit,
    down_lw,
    down_sw,
    up_lw,
    up_sw,
    flux,
    frac_col,
    solar_col,
    heat,
    gain,
):
    columns = index_ref.shape[1]
    slots = recv_ref.shape[0]
    g_lw, g_sw = table_lw_ref.shape[0], table_sw_ref.shape[0]
    g_all = g_lw + g_sw
    code = recv_ref[...].astype(I32) + 32768
    both = jnp.concatenate(
        [lax.shift_right_logical(code, 8).astype(F32).astype(BF16), (code & 255).astype(F32).astype(BF16)], axis=1
    )
    label = code[:, 3 * LEV : 3 * LEV + 1] - 0
    for k in range(columns // BLOCK):
        pick = one_hot(label, iota((slots, BLOCK), 1) + k * BLOCK)
        got = lax.dot_general(both, pick, TN, preferred_element_type=F32)
        value = got[: 4 * LEV] * 256.0 + got[4 * LEV :]
        for n, (low, width) in enumerate(CODES):
            phys[pl.ds(n * LEV, LEV), pl.ds(k * BLOCK, BLOCK)] = value[n * LEV : (n + 1) * LEV] * (width / 65535.0) + low
    planck = phys[0:LEV, :]
    path = phys[LEV : 2 * LEV, :]
    cloud = phys[2 * LEV : 3 * LEV, :]
    planck_ext[0:1, :] = jnp.zeros((1, columns), F32)
    planck_ext[pl.ds(1, LEV), :] = planck
    planck_ext[pl.ds(LEV + 1, 1), :] = surface_ref[...]
    ratio[...] = cloud / path
    for k in range(4):
        weights[pl.ds(k * LEV, LEV), :] = weight_ref[k].astype(F32)
    ones = jnp.where(iota((g_all, 128), 1) < 3, 1.0, 0.0).astype(BF16)
    table[:g_lw, :NTAB] = table_lw_ref[...]
    table[g_lw:, :NTAB] = table_sw_ref[...]
    table[:, NTAB:] = ones
    for mix in (mix_a, mix_b):
        mix[NTAB:, :] = jnp.zeros((KPAD - NTAB, GROUP * BLOCK), BF16)
    frac = jnp.sum(jnp.where(iota((g_lw, g_lw), 0) == iota((g_lw, g_lw), 1), frac_ref[...], 0.0), axis=1, keepdims=True)
    solar = jnp.sum(jnp.where(iota((g_sw, g_sw), 0) == iota((g_sw, g_sw), 1), solar_ref[...], 0.0), axis=1, keepdims=True)
    frac_col[...] = jnp.broadcast_to(frac, frac_col.shape)
    solar_col[...] = jnp.broadcast_to(solar, solar_col.shape)
    total = jnp.sum(frac_ref[...])
    levels = GROUP
    per_block = LEV // levels
    width = levels * BLOCK

    def place_of(q):
        base = pl.multiple_of(lax.shift_right_logical(q, per_block.bit_length() - 1) * BLOCK, BLOCK)
        return pl.ds(base, BLOCK), (q & (per_block - 1)) * levels

    def prepare(q, mix, out):
        here, first = place_of(q)
        for n in range(levels):
            level = first + n
            row = pl.ds(level, 1)
            lane = slice(n * BLOCK, (n + 1) * BLOCK)
            index = index_ref[row, here]
            temp = lax.shift_right_logical(index, 6).astype(F32).astype(BF16)
            press = index & 63
            w = [weights[pl.ds(c * LEV + level, 1), here] for c in range(4)]
            p_of = iota((PRESS, BLOCK), 0)
            at0, at1 = p_of == press, p_of == press + 1
            low = jnp.where(at0, w[0], jnp.where(at1, w[1], 0.0)).astype(BF16)
            wrap = (p_of == 0) & (press == PRESS - 1)
            high = jnp.where(at0, w[2], jnp.where(at1, w[3], jnp.where(wrap, w[1], 0.0))).astype(BF16)
            over = jnp.where(wrap, w[3], 0.0)[:16].astype(BF16)
            temps = jnp.broadcast_to(temp, (16, BLOCK))
            zero = jnp.zeros((16, BLOCK), BF16)
            is_temp = [temps == jnp.asarray(t, BF16) for t in range(TEMPS)]
            for t in range(TEMPS):
                for p in range(0, PRESS, 16):
                    tile = zero
                    if p == 0 and t >= 2:
                        tile = jnp.where(is_temp[t - 2], over, tile)
                    if t >= 1:
                        tile = jnp.where(is_temp[t - 1], high[p : p + 16], tile)
                    tile = jnp.where(is_temp[t], low[p : p + 16], tile)
                    mix[t * PRESS + p : t * PRESS + p + 16, lane] = tile
            pieces = split3(ratio[row, here])
            tail = [jnp.broadcast_to(x.astype(F32), (16, BLOCK)) for x in pieces]
            which = iota((16, BLOCK), 0)
            mix[NTAB : NTAB + 16, lane] = jnp.where(
                which == 0, tail[0], jnp.where(which == 1, tail[1], jnp.where(which == 2, tail[2], 0.0))
            ).astype(BF16)
        out[...] = jnp.dot(table[...], mix[...], preferred_element_type=F32)

    def enter_down(q):
        here, _ = place_of(q)
        down_lw[...] = jnp.zeros_like(down_lw)
        cosine = cosine_ref[:, here]
        top_beam = jnp.zeros((8, BLOCK), F32)
        for r in range(0, g_sw, 8):
            beam = solar_col[r : r + 8, :] * cosine
            down_sw[r : r + 8, :] = beam
            top_beam = top_beam + beam
        flux[0:1, :] = jnp.zeros((1, BLOCK), F32)
        flux[1:2, :] = jnp.sum(top_beam, axis=0, keepdims=True)

    def enter_up(q):
        here, _ = place_of(q)
        albedo = albedo_ref[:, here]
        ground_beam = flux[1:2, :]
        gain[0:1, here] = (1.0 - albedo) * ground_beam
        up_lw[...] = jnp.zeros_like(up_lw)
        for r in range(0, g_sw, 8):
            up_sw[r : r + 8, :] = down_sw[r : r + 8, :] * albedo
        flux[2:3, :] = surface_ref[:, here] * total
        flux[3:4, :] = ground_beam * albedo

    def downward(q, out):
        here, first = place_of(q)
        half = lax.shift_right_logical(q, per_block.bit_length() - 1) & 1
        inverse = -LOG2E / cosine_ref[:, here]
        diffuse, direct, step, own = [], [], [], []
        for n in range(levels):
            path_row = phys[pl.ds(LEV + first + n, 1), here]
            diffuse.append(path_row * DIFF)
            direct.append(path_row * inverse)
            own.append(planck_ext[pl.ds(first + n + 1, 1), here])
            step.append(planck_ext[pl.ds(first + n, 1), here] - own[-1])
        acc = [jnp.zeros((8, BLOCK), F32)] * levels
        for r in range(0, g_lw, 8):
            e = down_lw[r : r + 8, :]
            frac_here = frac_col[r : r + 8, :]
            for n in range(levels):
                t = jnp.exp2(out[r : r + 8, n * BLOCK : (n + 1) * BLOCK] * diffuse[n])
                transmit[half, first + n, r : r + 8, :] = t
                e = t * (e + step[n])
                acc[n] = acc[n] + e * frac_here
            down_lw[r : r + 8, :] = e
        acc_sw = [jnp.zeros((8, BLOCK), F32)] * levels
        for r in range(0, g_sw, 8):
            b = down_sw[r : r + 8, :]
            for n in range(levels):
                x = out[g_lw + r : g_lw + r + 8, n * BLOCK : (n + 1) * BLOCK]
                transmit[half, first + n, g_lw + r : g_lw + r + 8, :] = jnp.exp2(x * diffuse[n])
                b = b * jnp.exp2(x * direct[n])
                acc_sw[n] = acc_sw[n] + b
            down_sw[r : r + 8, :] = b
        lw, sw = flux[0:1, :], flux[1:2, :]
        for n in range(levels):
            new_lw = jnp.sum(acc[n], axis=0, keepdims=True) + own[n] * total
            new_sw = jnp.sum(acc_sw[n], axis=0, keepdims=True)
            heat[pl.ds(first + n, 1), here] = lw - new_lw
            heat[pl.ds(LEV + first + n, 1), here] = sw - new_sw
            lw, sw = new_lw, new_sw
        flux[0:1, :] = lw
        flux[1:2, :] = sw

    def upward(q):
        here, first = place_of(q)
        half = lax.shift_right_logical(q, per_block.bit_length() - 1) & 1
        last = LEV - 1 - first
        step, own = [], []
        for n in range(levels):
            own.append(planck_ext[pl.ds(last - n + 1, 1), here])
            step.append(planck_ext[pl.ds(last - n + 2, 1), here] - own[-1])
        acc = [jnp.zeros((8, BLOCK), F32)] * levels
        for r in range(0, g_lw, 8):
            e = up_lw[r : r + 8, :]
            frac_here = frac_col[r : r + 8, :]
            for n in range(levels):
                e = transmit[half, last - n, r : r + 8, :] * (e + step[n])
                acc[n] = acc[n] + e * frac_here
            up_lw[r : r + 8, :] = e
        acc_sw = [jnp.zeros((8, BLOCK), F32)] * levels
        for r in range(0, g_sw, 8):
            v = up_sw[r : r + 8, :]
            for n in range(levels):
                v = transmit[half, last - n, g_lw + r : g_lw + r + 8, :] * v
                acc_sw[n] = acc_sw[n] + v
            up_sw[r : r + 8, :] = v
        lw, sw = flux[2:3, :], flux[3:4, :]
        for n in range(levels):
            new_lw = jnp.sum(acc[n], axis=0, keepdims=True) + own[n] * total
            new_sw = jnp.sum(acc_sw[n], axis=0, keepdims=True)
            row, row_sw = pl.ds(last - n, 1), pl.ds(LEV + last - n, 1)
            heat[row, here] = heat[row, here] + (lw - new_lw)
            heat[row_sw, here] = heat[row_sw, here] + (sw - new_sw)
            lw, sw = new_lw, new_sw
        flux[2:3, :] = lw
        flux[3:4, :] = sw

    groups = per_block * (columns // BLOCK)

    def first_block(i, _):
        q = 2 * i
        prepare(q + 1, mix_b, out_b)
        downward(q, out_a)
        prepare(q + 2, mix_a, out_a)
        downward(q + 1, out_b)
        return 0

    def later_block(i, _):
        q = 2 * i

        @pl.when((q & (per_block - 1)) == 0)
        def _():
            enter_up(q - per_block)
            enter_down(q)

        upward(q - per_block)
        prepare(q + 1, mix_b, out_b)
        downward(q, out_a)
        upward(q + 1 - per_block)
        prepare(jnp.minimum(q + 2, groups - 1), mix_a, out_a)
        downward(q + 1, out_b)
        return 0

    def last_up(i, _):
        upward(i)
        return 0

    enter_down(0)
    prepare(0, mix_a, out_a)
    lax.fori_loop(0, per_block // 2, first_block, 0)
    lax.fori_loop(per_block // 2, groups // 2, later_block, 0)
    enter_up(groups - per_block)
    lax.fori_loop(groups - per_block, groups, last_up, 0)

    devices = slots // CAP
    half_rows = devices * CAP // 2
    sunlit = sunlit_ref[...]
    result = jnp.concatenate([heat[0:LEV, :], heat[LEV:, :] * sunlit.astype(F32)], axis=0)
    largest = jnp.max(jnp.abs(result), axis=1, keepdims=True)
    scale_code = jnp.ceil(jnp.log2(jnp.maximum(largest, 1e-30)) * 256.0 + 0.5)
    codes = result * (32767.0 * jnp.exp2(scale_code * (-1.0 / 256.0))) + 32768.5
    codes = jnp.clip(codes, 0.0, 65535.0).astype(I32)
    high = lax.shift_right_logical(codes, 8).astype(F32)
    low = (codes & 255).astype(F32)
    none = jnp.zeros_like(high)
    left = jnp.concatenate([high, none, low, none], axis=0).astype(BF16)
    right = jnp.concatenate([none, high, none, low], axis=0).astype(BF16)
    lanes = 4 * LEV
    diagonal = iota((2 * LEV, lanes), 0) == (iota((2 * LEV, lanes), 1) & (2 * LEV - 1))
    scale_row = jnp.sum(jnp.where(diagonal, scale_code, 0.0), axis=0, keepdims=True).astype(I32)

    sw_count = columns // 2
    sw_slot = slot_ref[...]
    owner = jnp.where(sunlit == 1, lax.shift_right_logical(sw_slot, sw_count.bit_length() - 1), owners)
    mark = jnp.where(iota((owners, columns), 0) == owner, 1.0, 0.0)
    place = owner * SW_CAP + dealt_rank(mark).astype(I32)
    scaled = gain[0:1, :] * (1.0 / GAIN_SCALE)
    first = jnp.floor(scaled * 32768.0)
    second = jnp.floor((scaled * 32768.0 - first) * 32768.0)
    first, second = first.astype(I32), second.astype(I32)
    own_slot = sw_slot & (sw_count - 1)
    pieces = [first, second, own_slot + 1]
    stack = jnp.zeros((16, columns), F32)
    at = iota((16, columns), 0)
    for n, x in enumerate(pieces):
        stack = jnp.where(at == 2 * n, lax.shift_right_logical(x, 8).astype(F32), stack)
        stack = jnp.where(at == 2 * n + 1, (x & 255).astype(F32), stack)
    stack = stack.astype(BF16)
    extras = []
    for o in range(0, owners, 2):
        pick = one_hot(iota((2 * SW_CAP, columns), 0) + o * SW_CAP, place)
        got = lax.dot_general(stack, pick, NT, preferred_element_type=F32)
        row_of = iota((8, lanes), 0)
        rows = [scale_row] + [
            (got[2 * n : 2 * n + 1] * 256.0 + got[2 * n + 1 : 2 * n + 2]).astype(I32) for n in range(3)
        ]
        both = jnp.zeros((8, lanes), I32)
        for n, x in enumerate(rows):
            both = jnp.where(row_of == n, x, both)
        extras += [both, both]
    extras = jnp.stack(extras)

    step = 256
    for k in range(half_rows // step):
        part = recv_ref[pl.ds(2 * k * step, 2 * step), :].astype(I32) + 32768
        label = jnp.broadcast_to(part[:, 3 * LEV : 3 * LEV + 1], (2 * step, 128)).reshape(2 * step // CAP, CAP, 128)
        got = jnp.zeros((step, 2 * lanes), F32)
        for side, value in enumerate((left, right)):
            mine = label[:, 8 * side : 8 * side + 8, :].reshape(step, 128)
            pick = jnp.concatenate(
                [one_hot(mine, iota((step, 128), 1) + c * 128) for c in range(columns // 128)], axis=1
            )
            got = got + lax.dot_general(pick, value, NT, preferred_element_type=F32)
        code = (got[:, :lanes] * 256.0 + got[:, lanes:]).astype(I32) - 32768
        code = code.reshape(step // 8, 8, lanes)
        more = jnp.concatenate([extras] * (step // 8 // owners), axis=0)
        out = jnp.concatenate([code, more], axis=1).reshape(2 * step, lanes)
        back_ref[pl.ds(2 * k * step, 2 * step), :] = out.astype(I16)


def home_kernel(back_ref, slot_ref, row_ref, lw_ref, sw_ref, surface_ref):
    columns = slot_ref.shape[1]
    slots = back_ref.shape[0]
    slot = slot_ref[...]
    got = jnp.zeros((4 * LEV, columns), F32)
    step = 256
    wide = 2 * LEV
    for k in range(slots // 2 // step):
        part = back_ref[pl.ds(2 * k * step, 2 * step), :].astype(I32).reshape(2 * step // CAP, CAP, 128)
        scale = jnp.exp2(part[:, 8:9, :].astype(F32) * (1.0 / 256.0)) * (1.0 / 32767.0)
        value = (part[:, :8, :].astype(F32) * scale).reshape(step, 128)
        first = value.astype(BF16)
        second = (value - first.astype(F32)).astype(BF16)
        row_of = iota((step, columns), 0) + k * step
        first_slot = lax.shift_right_logical(row_of, 3) * CAP + (row_of & 7)
        for side in range(2):
            pick = one_hot(first_slot + 8 * side, slot)
            lane = slice(side * wide, (side + 1) * wide)
            both = jnp.concatenate([first[:, lane], second[:, lane]], axis=1)
            got = got + lax.dot_general(both, pick, TN, preferred_element_type=F32)
    value = got[:wide] + got[wide:]
    lw_ref[...] = value[:LEV]
    sw_ref[...] = value[LEV:]

    count = surface_ref.shape[1]
    owners = 16
    mine = row_ref[0] * (owners * CAP)
    total = jnp.zeros((16, count), F32)
    odd = (row_ref[1] & 1) == 1
    for o in range(owners):
        got = back_ref[pl.ds(pl.multiple_of(mine + o * CAP, CAP), CAP), :].astype(I32)
        first, second, label = got[9:10], got[10:11], got[11:12]
        value = (first.astype(F32) + second.astype(F32) * (1.0 / 32768.0)) * (GAIN_SCALE / 32768.0)
        lane = iota((1, 128), 1)
        value = jnp.where((lane >= SW_CAP) == odd, value, 0.0)
        pick = one_hot(label - 1, iota((count, 128), 0))
        a, b, c = split3(value)
        at = iota((16, 128), 0)
        stack = jnp.where(
            at == 0, a.astype(F32), jnp.where(at == 1, b.astype(F32), jnp.where(at == 2, c.astype(F32), 0.0))
        )
        total = total + lax.dot_general(stack.astype(BF16), pick, NT, preferred_element_type=F32)
    surface_ref[...] = total[0:1] + total[1:2] + total[2:3]


def params():
    return pltpu.CompilerParams(vmem_limit_bytes=VMEM_LIMIT)


def vmem(count):
    return [pl.BlockSpec(memory_space=pltpu.VMEM)] * count


def body(
    planck_source,
    absorber_path,
    cloud_depth,
    span_map,
    surface_source,
    interp_index,
    interp_weight,
    sunlit,
    sw_slot,
    cos_zenith,
    albedo,
    table_lw,
    table_sw,
    planck_frac,
    solar_weight,
):
    columns = span_map.shape[0]
    owners = lax.axis_size("col")
    devices = lax.axis_size("dyn") * owners
    slots = devices * CAP
    g_lw, g_sw = table_lw.shape[0], table_sw.shape[0]

    def row(x):
        return x.reshape(1, -1)

    send, slot = pl.pallas_call(
        pack_kernel,
        out_shape=(jax.ShapeDtypeStruct((slots, 128), I16), jax.ShapeDtypeStruct((1, columns), I32)),
        in_specs=vmem(4),
        out_specs=tuple(vmem(2)),
        compiler_params=params(),
        name="pack",
    )(planck_source, absorber_path, cloud_depth, row(span_map))
    recv = lax.all_to_all(send.reshape(devices, CAP, 128), ("dyn", "col"), 0, 0, tiled=True)
    back = pl.pallas_call(
        partial(radiation_kernel, owners),
        out_shape=jax.ShapeDtypeStruct((slots, 128), I16),
        in_specs=vmem(12),
        out_specs=vmem(1)[0],
        scratch_shapes=[
            pltpu.VMEM((3 * LEV, columns), F32),
            pltpu.VMEM((4 * LEV, columns), F32),
            pltpu.VMEM((40, columns), F32),
            pltpu.VMEM((LEV, columns), F32),
            pltpu.VMEM((g_lw + g_sw, KPAD), BF16),
            pltpu.VMEM((KPAD, GROUP * BLOCK), BF16),
            pltpu.VMEM((KPAD, GROUP * BLOCK), BF16),
            pltpu.VMEM((g_lw + g_sw, GROUP * BLOCK), F32),
            pltpu.VMEM((g_lw + g_sw, GROUP * BLOCK), F32),
            pltpu.VMEM((2, LEV, g_lw + g_sw, BLOCK), F32),
            pltpu.VMEM((g_lw, BLOCK), F32),
            pltpu.VMEM((g_sw, BLOCK), F32),
            pltpu.VMEM((g_lw, BLOCK), F32),
            pltpu.VMEM((g_sw, BLOCK), F32),
            pltpu.VMEM((8, BLOCK), F32),
            pltpu.VMEM((g_lw, BLOCK), F32),
            pltpu.VMEM((g_sw, BLOCK), F32),
            pltpu.VMEM((2 * LEV, columns), F32),
            pltpu.VMEM((8, columns), F32),
        ],
        compiler_params=params(),
        name="radiation",
    )(
        recv.reshape(slots, 128),
        row(surface_source),
        interp_index,
        interp_weight,
        row(sunlit),
        row(sw_slot),
        row(cos_zenith),
        row(albedo),
        table_lw,
        table_sw,
        row(planck_frac),
        row(solar_weight),
    )
    home = lax.all_to_all(back.reshape(devices, CAP, 128), ("dyn", "col"), 0, 0, tiled=True)
    place = jnp.stack([lax.axis_index("dyn"), lax.axis_index("col")]).astype(I32)
    heating_lw, heating_sw, surface = pl.pallas_call(
        home_kernel,
        out_shape=(jax.ShapeDtypeStruct((LEV, columns), F32),) * 2
        + (jax.ShapeDtypeStruct((1, columns // 2), F32),),
        in_specs=vmem(2) + [pl.BlockSpec(memory_space=pltpu.SMEM)],
        out_specs=tuple(vmem(3)),
        compiler_params=params(),
        name="home",
    )(home.reshape(slots, 128), slot, place)
    return (heating_lw, heating_sw, surface.reshape(-1))


def solution(mesh):
    columns = P(None, ("dyn", "col"))
    flat = P(("dyn", "col"))
    in_specs = (
        columns, columns, columns, flat, flat, columns, P(None, None, ("dyn", "col")),
        flat, flat, flat, flat, P(), P(), P(), P(),
    )
    out_specs = (columns, columns, flat)
    return jax.shard_map(body, mesh=mesh, in_specs=in_specs, out_specs=out_specs, check_vma=False)
```

time: 142 us -> 108 us (0.76)
  Pallas kernels: 86.8 us -> 62.3 us
  blocking collectives: 36.3 us -> 25.7 us
  waiting for transfers between devices: 12.1 us -> 13.6 us
    pallas_call x2 -> x1, Pallas kernels: 80.9 us -> 55.4 us  [body(): pl.pallas_call(partial(radiation_kernel, owners), out_shape=jax.ShapeDtyp...]
    all_to_all x1 -> x0, blocking collectives: 10.6 us -> none  [body(): ground_in = lax.all_to_all(ground, 'col', 0, 0, tiled=True)]
    all_to_all x1, waiting for transfers between devices: 12.1 us -> 13.6 us  [body(): lax.all_to_all(back.reshape(devices, CAP, 128), ('dyn', 'col'), 0, 0, til...]
  transfers between devices with their start and end apart: 1 -> 1, of which waited for: 1 -> 1; matrix products, arithmetic and copies ran while one was open for 0% -> 1% of each run, Pallas kernels for 1% -> 0%
where the time goes in v2:
time: 108 us
  Pallas kernels  62.3 us (58%)
  blocking collectives  25.7 us (24%)
  waiting for transfers between devices  13.6 us (13%)
  starting transfers between devices  4 us (4%)
    pallas_call x1, Pallas kernels, body(): pl.pallas_call(partial(radiation_kernel, owners), out_shape=jax.ShapeDtyp...  55.4 us
    all_to_all x1, blocking collectives, body(): lax.all_to_all(send.reshape(devices, CAP, 128), ('dyn', 'col'), 0, 0, til...  25.7 us
    all_to_all x1, waiting for transfers between devices, body(): lax.all_to_all(back.reshape(devices, CAP, 128), ('dyn', 'col'), 0, 0, til...  13.6 us
    all_to_all x1, starting transfers between devices, body(): lax.all_to_all(back.reshape(devices, CAP, 128), ('dyn', 'col'), 0, 0, til...  4 us
    pallas_call x1, Pallas kernels, body(): pl.pallas_call(home_kernel, out_shape=(jax.ShapeDtypeStruct((LEV, columns...  3.48 us
    pallas_call x1, Pallas kernels, body(): pl.pallas_call(pack_kernel, out_shape=(jax.ShapeDtypeStruct((slots, 128),...  3.35 us
  transfers between devices with their start and end apart: 1, of which 1 were waited for; matrix products, arithmetic and copies ran while one was open for 1% of the time, Pallas kernels for 0%

profile of v2, /device:TPU:1, one launch (start us, length us, event | category | flops | bytes accessed | tf_op | source)
XLA Modules:
  0.0 107.6 jit_solution(18190143625854444113)
XLA Ops:
  0.6 3.4 %pack.1 = (s16[2048,128]{1,0:T(8,128)(2,1)}, s32[1,1024]{1,0:T(1,128)}) custom-call(f32[32,1024]{1,0:T(8,128)} %planck_ref.1, f32[32,1024]{1,0:T(8,128)} %path_ref.1, f32[32,1024]{1,0:T(8,128)} %cloud_ref.1, s32[1,1024]{1,0:T(1,128)} %bitcast.19), custom_call_target="tpu_custom_call" | custom-call | tf_op jit(solution)/shard_map/pack/pallas_call | solution.py:480
  4.0 25.7 %all_to_all.10 = s16[128,16,128]{2,1,0:T(8,128)(2,1)} all-to-all(s16[128,16,128]{2,1,0:T(8,128)(2,1)} %bitcast.18), channel_id=1, replica_groups=mesh['dyn'=8,'col'=16] {'dyn','col'}, dimensions={0} | all-to-all | bytes 1048576 | tf_op jit(solution)/shard_map/all_to_all | solution.py:488
  29.7 55.4 %radiation.1 = s16[2048,128]{1,0:T(8,128)(2,1)} custom-call(s16[2048,128]{1,0:T(8,128)(2,1)} %bitcast.17, f32[1,1024]{1,0:T(1,128)} %bitcast.20, s32[32,1024]{1,0:T(8,128)} %index_ref.1, bf16[4,32,1024]{2,1,0:T(8,128)(2,1)} %weight_ref.1, s32[1,1024]{1,0:T(1,128)} %bitcast.21, s32[1,1024]{1,0:T(1,128)} %bitcast.22, f32[1,1024]{1,0:T(1,128)} %bitcast.23, ...), custom_call_target="tpu_custom_call" | custom-call | tf_op jit(solution)/shard_map/radiation/pallas_call | solution.py:489
  85.1 4.0 %all-to-all-start.1 = ((s16[128,16,128]{2,1,0:T(8,128)(2,1)}), s16[128,16,128]{2,1,0:T(8,128)(2,1)S(1)}, u32[]{:S(2)}, u32[]{:S(2)}) async-start(s16[128,16,128]{2,1,0:T(8,128)(2,1)} %bitcast.16), calls=%async_computation.1 | async-start | bytes 1048576 | tf_op jit(solution)/shard_map/all_to_all | solution.py:531
  89.1 0.7 pad_add_fusion.row_ref
  89.8 13.6 %all-to-all-done.1 = s16[128,16,128]{2,1,0:T(8,128)(2,1)S(1)} async-done(((s16[128,16,128]{2,1,0:T(8,128)(2,1)}), s16[128,16,128]{2,1,0:T(8,128)(2,1)S(1)}, u32[]{:S(2)}, u32[]{:S(2)}) %all-to-all-start.1) | async-done | bytes 524320 | tf_op jit(solution)/shard_map/all_to_all | solution.py:531
  103.3 0.0 copy-start
  103.3 0.8 copy-done
  104.1 3.5 %home.1 = (f32[32,1024]{1,0:T(8,128)}, f32[32,1024]{1,0:T(8,128)}, f32[1,512]{1,0:T(1,128)}) custom-call(s16[2048,128]{1,0:T(8,128)(2,1)} %bitcast.15, s32[1,1024]{1,0:T(1,128)} %get-tuple-element.9.slot_ref, s32[2]{0:T(128)} %pad_add_fusion.row_ref), custom_call_target="tpu_custom_call" | custom-call | tf_op jit(solution)/shard_map/home/pallas_call | solution.py:533
Async XLA Ops:
  85.1 18.2 %all-to-all-start.1 = ((s16[128,16,128]{2,1,0:T(8,128)(2,1)}), s16[128,16,128]{2,1,0:T(8,128)(2,1)S(1)}, u32[]{:S(2)}, u32[]{:S(2)}) async-start(s16[128,16,128]{2,1,0:T(8,128)(2,1)} %bitcast.16), calls=%async_computation.1 | async-start | bytes 1048576 | tf_op jit(solution)/shard_map/all_to_all | solution.py:531
  103.3 0.8 copy-start

commit v3 on v2

--- a/solution.py
+++ b/solution.py
@@ -19,6 +19,7 @@
 CODES = ((0.5, 1.0), (0.2, 2.8), (0.0, 0.6))
 BLOCK = 256
 GROUP = 4
+EARLY = 2
 VMEM_LIMIT = 60 * 1024 * 1024
 NT = (((1,), (1,)), ((), ()))
 TN = (((0,), (0,)), ((), ()))
@@ -55,6 +56,66 @@
 
 def one_hot_less():
     return jnp.where(iota((128, 128), 0) < iota((128, 128), 1), 1.0, 0.0).astype(BF16)
+
+
+def mix_level(index, weight_rows, mix, lane):
+    wide = index.shape[1]
+
+    def spread(x):
+        return jnp.broadcast_to(x.astype(F32).astype(BF16), (16, wide))
+
+    temp = spread(lax.shift_right_logical(index, 6))
+    press = spread(index & (PRESS - 1))
+    after = press + jnp.asarray(1, BF16)
+    w = [spread(x) for x in weight_rows]
+    zero = jnp.zeros((16, wide), BF16)
+    at = iota((16, wide), 0).astype(F32).astype(BF16)
+    low, high = [], []
+    for p in range(0, PRESS, 16):
+        here = at + jnp.asarray(p, BF16)
+        at0, at1 = here == press, here == after
+        low.append(jnp.where(at0, w[0], jnp.where(at1, w[1], zero)))
+        high.append(jnp.where(at0, w[2], jnp.where(at1, w[3], zero)))
+    wrap = at == press - jnp.asarray(PRESS - 1, BF16)
+    high[0] = jnp.where(wrap, w[1], high[0])
+    over = jnp.where(wrap, w[3], zero)
+    for t in range(TEMPS):
+        is_temp = [temp == jnp.asarray(t - d, BF16) for d in range(3)]
+        for n in range(PRESS // 16):
+            tile = zero
+            if n == 0 and t >= 2:
+                tile = jnp.where(is_temp[2], over, tile)
+            if t >= 1:
+                tile = jnp.where(is_temp[1], high[n], tile)
+            tile = jnp.where(is_temp[0], low[n], tile)
+            first = t * PRESS + n * 16
+            mix[first : first + 16, lane] = tile
+
+
+def absorb_kernel(index_ref, weight_ref, table_lw_ref, table_sw_ref, out_ref, weights, table, mix):
+    g_lw = table_lw_ref.shape[0]
+    step = pl.program_id(0)
+
+    @pl.when(step == 0)
+    def _():
+        for k in range(4):
+            weights[pl.ds(k * LEV, LEV), :] = weight_ref[k].astype(F32)
+        table[:g_lw, :] = table_lw_ref[...]
+        table[g_lw:, :] = table_sw_ref[...]
+
+    units = out_ref.shape[0]
+    for u in range(units):
+        unit = step * units + u
+        per = LEV // (2 * GROUP)
+        here = pl.ds(pl.multiple_of(unit // per * BLOCK, BLOCK), BLOCK)
+        for n in range(EARLY):
+            level = (unit % per) * 2 * GROUP + 2 * GROUP - EARLY + n
+            row = pl.ds(level, 1)
+            lane = slice((u * EARLY + n) * BLOCK, (u * EARLY + n + 1) * BLOCK)
+            mix_level(index_ref[row, here], [weights[pl.ds(c * LEV + level, 1), here] for c in range(4)], mix, lane)
+    got = jnp.dot(table[...], mix[...], preferred_element_type=F32)
+    for u in range(units):
+        out_ref[u] = got[:, u * EARLY * BLOCK : (u + 1) * EARLY * BLOCK]
 
 
 def pack_kernel(planck_ref, path_ref, cloud_ref, map_ref, send_ref, slot_ref):
@@ -87,6 +148,7 @@
 def radiation_kernel(
     owners,
     recv_ref,
+    pre_ref,
     surface_ref,
     index_ref,
     weight_ref,
@@ -118,11 +180,15 @@
     solar_col,
     heat,
     gain,
+    pre_buf,
+    pre_sem,
 ):
     columns = index_ref.shape[1]
     slots = recv_ref.shape[0]
     g_lw, g_sw = table_lw_ref.shape[0], table_sw_ref.shape[0]
     g_all = g_lw + g_sw
+    first_fetch = pltpu.make_async_copy(pre_ref.at[0], pre_buf.at[0], pre_sem.at[0])
+    first_fetch.start()
     code = recv_ref[...].astype(I32) + 32768
     both = jnp.concatenate(
         [lax.shift_right_logical(code, 8).astype(F32).astype(BF16), (code & 255).astype(F32).astype(BF16)], axis=1
@@ -148,7 +214,7 @@
     table[g_lw:, :NTAB] = table_sw_ref[...]
     table[:, NTAB:] = ones
     for mix in (mix_a, mix_b):
-        mix[NTAB:, :] = jnp.zeros((KPAD - NTAB, GROUP * BLOCK), BF16)
+        mix[NTAB:, :] = jnp.zeros((KPAD - NTAB, mix.shape[1]), BF16)
     frac = jnp.sum(jnp.where(iota((g_lw, g_lw), 0) == iota((g_lw, g_lw), 1), frac_ref[...], 0.0), axis=1, keepdims=True)
     solar = jnp.sum(jnp.where(iota((g_sw, g_sw), 0) == iota((g_sw, g_sw), 1), solar_ref[...], 0.0), axis=1, keepdims=True)
     frac_col[...] = jnp.broadcast_to(frac, frac_col.shape)
@@ -162,34 +228,13 @@
         base = pl.multiple_of(lax.shift_right_logical(q, per_block.bit_length() - 1) * BLOCK, BLOCK)
         return pl.ds(base, BLOCK), (q & (per_block - 1)) * levels
 
-    def prepare(q, mix, out):
+    def prepare(q, mix, out, count=GROUP):
         here, first = place_of(q)
-        for n in range(levels):
+        for n in range(count):
             level = first + n
             row = pl.ds(level, 1)
             lane = slice(n * BLOCK, (n + 1) * BLOCK)
-            index = index_ref[row, here]
-            temp = lax.shift_right_logical(index, 6).astype(F32).astype(BF16)
-            press = index & 63
-            w = [weights[pl.ds(c * LEV + level, 1), here] for c in range(4)]
-            p_of = iota((PRESS, BLOCK), 0)
-            at0, at1 = p_of == press, p_of == press + 1
-            low = jnp.where(at0, w[0], jnp.where(at1, w[1], 0.0)).astype(BF16)
-            wrap = (p_of == 0) & (press == PRESS - 1)
-            high = jnp.where(at0, w[2], jnp.where(at1, w[3], jnp.where(wrap, w[1], 0.0))).astype(BF16)
-            over = jnp.where(wrap, w[3], 0.0)[:16].astype(BF16)
-            temps = jnp.broadcast_to(temp, (16, BLOCK))
-            zero = jnp.zeros((16, BLOCK), BF16)
-            is_temp = [temps == jnp.asarray(t, BF16) for t in range(TEMPS)]
-            for t in range(TEMPS):
-                for p in range(0, PRESS, 16):
-                    tile = zero
-                    if p == 0 and t >= 2:
-                        tile = jnp.where(is_temp[t - 2], over, tile)
-                    if t >= 1:
-                        tile = jnp.where(is_temp[t - 1], high[p : p + 16], tile)
-                    tile = jnp.where(is_temp[t], low[p : p + 16], tile)
-                    mix[t * PRESS + p : t * PRESS + p + 16, lane] = tile
+            mix_level(index_ref[row, here], [weights[pl.ds(c * LEV + level, 1), here] for c in range(4)], mix, lane)
             pieces = split3(ratio[row, here])
             tail = [jnp.broadcast_to(x.astype(F32), (16, BLOCK)) for x in pieces]
             which = iota((16, BLOCK), 0)
@@ -221,10 +266,18 @@
         flux[2:3, :] = surface_ref[:, here] * total
         flux[3:4, :] = ground_beam * albedo
 
-    def downward(q, out):
+    def downward(q, out, early=None):
         here, first = place_of(q)
         half = lax.shift_right_logical(q, per_block.bit_length() - 1) & 1
         inverse = -LOG2E / cosine_ref[:, here]
+        ready = levels if early is None else levels - EARLY
+        extra = [ratio[pl.ds(first + n, 1), here] for n in range(ready, levels)]
+
+        def absorbed(r, n):
+            if n < ready:
+                return out[r : r + 8, n * BLOCK : (n + 1) * BLOCK]
+            return pre_buf[early, r : r + 8, (n - ready) * BLOCK : (n - ready + 1) * BLOCK] + extra[n - ready]
+
         diffuse, direct, step, own = [], [], [], []
         for n in range(levels):
             path_row = phys[pl.ds(LEV + first + n, 1), here]
@@ -237,7 +290,7 @@
             e = down_lw[r : r + 8, :]
             frac_here = frac_col[r : r + 8, :]
             for n in range(levels):
-                t = jnp.exp2(out[r : r + 8, n * BLOCK : (n + 1) * BLOCK] * diffuse[n])
+                t = jnp.exp2(absorbed(r, n) * diffuse[n])
                 transmit[half, first + n, r : r + 8, :] = t
                 e = t * (e + step[n])
                 acc[n] = acc[n] + e * frac_here
@@ -246,7 +299,7 @@
         for r in range(0, g_sw, 8):
             b = down_sw[r : r + 8, :]
             for n in range(levels):
-                x = out[g_lw + r : g_lw + r + 8, n * BLOCK : (n + 1) * BLOCK]
+                x = absorbed(g_lw + r, n)
                 transmit[half, first + n, g_lw + r : g_lw + r + 8, :] = jnp.exp2(x * diffuse[n])
                 b = b * jnp.exp2(x * direct[n])
                 acc_sw[n] = acc_sw[n] + b
@@ -297,16 +350,28 @@
 
     groups = per_block * (columns // BLOCK)
 
+    def fetch(i):
+        return pltpu.make_async_copy(pre_ref.at[i], pre_buf.at[i & 1], pre_sem.at[i & 1])
+
+    def turn(i):
+        fetch(i).wait()
+
+        @pl.when(i + 1 < groups // 2)
+        def _():
+            fetch(i + 1).start()
+
     def first_block(i, _):
         q = 2 * i
-        prepare(q + 1, mix_b, out_b)
+        turn(i)
+        prepare(q + 1, mix_b, out_b, levels - EARLY)
         downward(q, out_a)
         prepare(q + 2, mix_a, out_a)
-        downward(q + 1, out_b)
+        downward(q + 1, out_b, i & 1)
         return 0
 
     def later_block(i, _):
         q = 2 * i
+        turn(i)
 
         @pl.when((q & (per_block - 1)) == 0)
         def _():
@@ -314,11 +379,11 @@
             enter_down(q)
 
         upward(q - per_block)
-        prepare(q + 1, mix_b, out_b)
+        prepare(q + 1, mix_b, out_b, levels - EARLY)
         downward(q, out_a)
         upward(q + 1 - per_block)
         prepare(jnp.minimum(q + 2, groups - 1), mix_a, out_a)
-        downward(q + 1, out_b)
+        downward(q + 1, out_b, i & 1)
         return 0
 
     def last_up(i, _):
@@ -485,11 +550,32 @@
         compiler_params=params(),
         name="pack",
     )(planck_source, absorber_path, cloud_depth, row(span_map))
+    early_units = LEV // (2 * GROUP) * (columns // BLOCK)
+    units = 4 // EARLY
+    early = pl.pallas_call(
+        absorb_kernel,
+        grid=(early_units // units,),
+        out_shape=jax.ShapeDtypeStruct((early_units, g_lw + g_sw, EARLY * BLOCK), F32),
+        in_specs=vmem(4),
+        out_specs=pl.BlockSpec((units, g_lw + g_sw, EARLY * BLOCK), lambda i: (i, 0, 0)),
+        scratch_shapes=[
+            pltpu.VMEM((4 * LEV, columns), F32),
+            pltpu.VMEM((g_lw + g_sw, NTAB), BF16),
+            pltpu.VMEM((NTAB, units * EARLY * BLOCK), BF16),
+        ],
+        compiler_params=params(),
+        cost_estimate=pl.CostEstimate(
+            flops=2 * (g_lw + g_sw) * NTAB * early_units * EARLY * BLOCK,
+            bytes_accessed=4 * (g_lw + g_sw) * early_units * EARLY * BLOCK,
+            transcendentals=0,
+        ),
+        name="absorb",
+    )(interp_index, interp_weight, table_lw, table_sw)
     recv = lax.all_to_all(send.reshape(devices, CAP, 128), ("dyn", "col"), 0, 0, tiled=True)
     back = pl.pallas_call(
         partial(radiation_kernel, owners),
         out_shape=jax.ShapeDtypeStruct((slots, 128), I16),
-        in_specs=vmem(12),
+        in_specs=vmem(1) + [pl.BlockSpec(memory_space=pl.ANY)] + vmem(11),
         out_specs=vmem(1)[0],
         scratch_shapes=[
             pltpu.VMEM((3 * LEV, columns), F32),
@@ -498,9 +584,9 @@
             pltpu.VMEM((LEV, columns), F32),
             pltpu.VMEM((g_lw + g_sw, KPAD), BF16),
             pltpu.VMEM((KPAD, GROUP * BLOCK), BF16),
-            pltpu.VMEM((KPAD, GROUP * BLOCK), BF16),
+            pltpu.VMEM((KPAD, (GROUP - EARLY) * BLOCK), BF16),
             pltpu.VMEM((g_lw + g_sw, GROUP * BLOCK), F32),
-            pltpu.VMEM((g_lw + g_sw, GROUP * BLOCK), F32),
+            pltpu.VMEM((g_lw + g_sw, (GROUP - EARLY) * BLOCK), F32),
             pltpu.VMEM((2, LEV, g_lw + g_sw, BLOCK), F32),
             pltpu.VMEM((g_lw, BLOCK), F32),
             pltpu.VMEM((g_sw, BLOCK), F32),
@@ -511,11 +597,14 @@
             pltpu.VMEM((g_sw, BLOCK), F32),
             pltpu.VMEM((2 * LEV, columns), F32),
             pltpu.VMEM((8, columns), F32),
+            pltpu.VMEM((2, g_lw + g_sw, EARLY * BLOCK), F32),
+            pltpu.SemaphoreType.DMA((2,)),
         ],
         compiler_params=params(),
         name="radiation",
     )(
         recv.reshape(slots, 128),
+        early,
         row(surface_source),
         interp_index,
         interp_weight,

time: 108 us -> 107 us (level)
  blocking collectives: 25.7 us -> 0 us
  starting transfers between devices: 4 us -> 19.9 us
  Pallas kernels: 62.3 us -> 69.4 us
  waiting for transfers between devices: 13.6 us -> 14.8 us
    all_to_all x1 -> x0, blocking collectives: 25.7 us -> none  [body(): lax.all_to_all(send.reshape(devices, CAP, 128), ('dyn', 'col'), 0, 0, til...]
    pallas_call x0 -> x1, Pallas kernels: none -> 12.7 us  [body(): pl.pallas_call(absorb_kernel, grid=(early_units // units,), out_shape=jax...]
    all_to_all x0 -> x1, starting transfers between devices: none -> 11.5 us  [body(): lax.all_to_all(send.reshape(devices, CAP, 128), ('dyn', 'col'), 0, 0, til...]
    pallas_call x1, Pallas kernels: 55.4 us -> 49.9 us  [body(): pl.pallas_call(partial(radiation_kernel, owners), out_shape=jax.ShapeDtyp...]
    all_to_all x1, starting transfers between devices: 4 us -> 8.44 us  [body(): lax.all_to_all(back.reshape(devices, CAP, 128), ('dyn', 'col'), 0, 0, til...]
    all_to_all x0 -> x1, waiting for transfers between devices: none -> 1.34 us  [body(): lax.all_to_all(send.reshape(devices, CAP, 128), ('dyn', 'col'), 0, 0, til...]
  transfers between devices with their start and end apart: 1 -> 2, of which waited for: 1 -> 2; matrix products, arithmetic and copies ran while one was open for 1% -> 1% of each run, Pallas kernels for 0% -> 12%
where the time goes in v3:
time: 107 us
  Pallas kernels  69.4 us (65%)
  starting transfers between devices  19.9 us (19%)
  waiting for transfers between devices  14.8 us (14%)
  local copies, waits for them, and re-layouts  1.6 us (1%)
    pallas_call x1, Pallas kernels, body(): pl.pallas_call(partial(radiation_kernel, owners), out_shape=jax.ShapeDtyp...  49.9 us
    all_to_all x1, waiting for transfers between devices, body(): lax.all_to_all(back.reshape(devices, CAP, 128), ('dyn', 'col'), 0, 0, til...  13.4 us
    pallas_call x1, Pallas kernels, body(): pl.pallas_call(absorb_kernel, grid=(early_units // units,), out_shape=jax...  12.7 us
    all_to_all x1, starting transfers between devices, body(): lax.all_to_all(send.reshape(devices, CAP, 128), ('dyn', 'col'), 0, 0, til...  11.5 us
    all_to_all x1, starting transfers between devices, body(): lax.all_to_all(back.reshape(devices, CAP, 128), ('dyn', 'col'), 0, 0, til...  8.44 us
    pallas_call x1, Pallas kernels, body(): pl.pallas_call(home_kernel, out_shape=(jax.ShapeDtypeStruct((LEV, columns...  3.49 us
    pallas_call x1, Pallas kernels, body(): pl.pallas_call(pack_kernel, out_shape=(jax.ShapeDtypeStruct((slots, 128),...  3.35 us
  transfers between devices with their start and end apart: 2, of which 2 were waited for; matrix products, arithmetic and copies ran while one was open for 1% of the time, Pallas kernels for 12%

profile of v3, /device:TPU:1, one launch (start us, length us, event | category | flops | bytes accessed | tf_op | source)
XLA Modules:
  0.0 107.0 jit_solution(12711080257288899528)
XLA Ops:
  0.6 3.3 %pack.1 = (s16[2048,128]{1,0:T(8,128)(2,1)}, s32[1,1024]{1,0:T(1,128)}) custom-call(f32[32,1024]{1,0:T(8,128)} %planck_ref.1, f32[32,1024]{1,0:T(8,128)} %path_ref.1, f32[32,1024]{1,0:T(8,128)} %cloud_ref.1, s32[1,1024]{1,0:T(1,128)} %bitcast.19), custom_call_target="tpu_custom_call" | custom-call | tf_op jit(solution)/shard_map/pack/pallas_call | solution.py:545
  4.0 11.5 %all-to-all-start = ((s16[128,16,128]{2,1,0:T(8,128)(2,1)}), s16[128,16,128]{2,1,0:T(8,128)(2,1)S(1)}, u32[]{:S(2)}, u32[]{:S(2)}) async-start(s16[128,16,128]{2,1,0:T(8,128)(2,1)} %bitcast.18), calls=%async_computation | async-start | bytes 1048576 | tf_op jit(solution)/shard_map/all_to_all | solution.py:574
  15.5 12.7 %absorb.1.pre_ref = f32[16,480,512]{2,1,0:T(8,128)} custom-call(s32[32,1024]{1,0:T(8,128)} %index_ref.3, bf16[4,32,1024]{2,1,0:T(8,128)(2,1)} %weight_ref.3, bf16[256,896]{1,0:T(8,128)(2,1)} %table_lw_ref.3, bf16[224,896]{1,0:T(8,128)(2,1)} %table_sw_ref.3), custom_call_target="tpu_custom_call" | custom-call | flops 7046430720 | bytes 15728640 | tf_op jit(solution)/shard_map/absorb/pallas_call | solution.py:555
  28.2 1.3 %all-to-all-done = s16[128,16,128]{2,1,0:T(8,128)(2,1)S(1)} async-done(((s16[128,16,128]{2,1,0:T(8,128)(2,1)}), s16[128,16,128]{2,1,0:T(8,128)(2,1)S(1)}, u32[]{:S(2)}, u32[]{:S(2)}) %all-to-all-start) | async-done | bytes 524320 | tf_op jit(solution)/shard_map/all_to_all | solution.py:574
  29.6 0.0 copy-start
  29.6 0.8 copy-done
  30.4 49.9 %radiation.1 = s16[2048,128]{1,0:T(8,128)(2,1)} custom-call(s16[2048,128]{1,0:T(8,128)(2,1)} %bitcast.16, f32[16,480,512]{2,1,0:T(8,128)} %absorb.1.pre_ref, f32[1,1024]{1,0:T(1,128)} %bitcast.20, s32[32,1024]{1,0:T(8,128)} %index_ref.3, bf16[4,32,1024]{2,1,0:T(8,128)(2,1)} %weight_ref.3, s32[1,1024]{1,0:T(1,128)} %bitcast.21, s32[1,1024]{1,0:T(1,128)} %bitcast.22, ...), custom_call_target="tpu_custom_call" | custom-call | tf_op jit(solution)/shard_map/radiation/pallas_call | solution.py:575
  80.2 8.4 %all-to-all-start.1 = ((s16[128,16,128]{2,1,0:T(8,128)(2,1)}), s16[128,16,128]{2,1,0:T(8,128)(2,1)S(1)}, u32[]{:S(2)}, u32[]{:S(2)}) async-start(s16[128,16,128]{2,1,0:T(8,128)(2,1)} %bitcast.15), calls=%async_computation.1 | async-start | bytes 1048576 | tf_op jit(solution)/shard_map/all_to_all | solution.py:620
  88.7 0.7 pad_add_fusion.row_ref
  89.3 13.4 %all-to-all-done.1 = s16[128,16,128]{2,1,0:T(8,128)(2,1)S(1)} async-done(((s16[128,16,128]{2,1,0:T(8,128)(2,1)}), s16[128,16,128]{2,1,0:T(8,128)(2,1)S(1)}, u32[]{:S(2)}, u32[]{:S(2)}) %all-to-all-start.1) | async-done | bytes 524320 | tf_op jit(solution)/shard_map/all_to_all | solution.py:620
  102.8 0.0 copy-start.1
  102.8 0.8 copy-done.1
  103.5 3.5 %home.1 = (f32[32,1024]{1,0:T(8,128)}, f32[32,1024]{1,0:T(8,128)}, f32[1,512]{1,0:T(1,128)}) custom-call(s16[2048,128]{1,0:T(8,128)(2,1)} %bitcast.17, s32[1,1024]{1,0:T(1,128)} %get-tuple-element.9.slot_ref, s32[2]{0:T(128)} %pad_add_fusion.row_ref), custom_call_target="tpu_custom_call" | custom-call | tf_op jit(solution)/shard_map/home/pallas_call | solution.py:622
Async XLA Ops:
  4.0 25.6 %all-to-all-start = ((s16[128,16,128]{2,1,0:T(8,128)(2,1)}), s16[128,16,128]{2,1,0:T(8,128)(2,1)S(1)}, u32[]{:S(2)}, u32[]{:S(2)}) async-start(s16[128,16,128]{2,1,0:T(8,128)(2,1)} %bitcast.18), calls=%async_computation | async-start | bytes 1048576 | tf_op jit(solution)/shard_map/all_to_all | solution.py:574
  29.6 0.8 copy-start
  80.2 22.5 %all-to-all-start.1 = ((s16[128,16,128]{2,1,0:T(8,128)(2,1)}), s16[128,16,128]{2,1,0:T(8,128)(2,1)S(1)}, u32[]{:S(2)}, u32[]{:S(2)}) async-start(s16[128,16,128]{2,1,0:T(8,128)(2,1)} %bitcast.15), calls=%async_computation.1 | async-start | bytes 1048576 | tf_op jit(solution)/shard_map/all_to_all | solution.py:620
  102.8 0.8 copy-start.1

commit v4 on v3

--- a/solution.py
+++ b/solution.py
@@ -19,8 +19,8 @@
 CODES = ((0.5, 1.0), (0.2, 2.8), (0.0, 0.6))
 BLOCK = 256
 GROUP = 4
-EARLY = 2
-VMEM_LIMIT = 60 * 1024 * 1024
+EARLY = 1
+MIB = 1024 * 1024
 NT = (((1,), (1,)), ((), ()))
 TN = (((0,), (0,)), ((), ()))
 
@@ -463,7 +463,7 @@
         back_ref[pl.ds(2 * k * step, 2 * step), :] = out.astype(I16)
 
 
-def home_kernel(back_ref, slot_ref, row_ref, lw_ref, sw_ref, surface_ref):
+def home_kernel(back_ref, slot_ref, lw_ref, sw_ref, surface_ref):
     columns = slot_ref.shape[1]
     slots = back_ref.shape[0]
     slot = slot_ref[...]
@@ -489,9 +489,9 @@
 
     count = surface_ref.shape[1]
     owners = 16
-    mine = row_ref[0] * (owners * CAP)
+    mine = lax.axis_index("dyn") * (owners * CAP)
     total = jnp.zeros((16, count), F32)
-    odd = (row_ref[1] & 1) == 1
+    odd = (lax.axis_index("col") & 1) == 1
     for o in range(owners):
         got = back_ref[pl.ds(pl.multiple_of(mine + o * CAP, CAP), CAP), :].astype(I32)
         first, second, label = got[9:10], got[10:11], got[11:12]
@@ -508,8 +508,8 @@
     surface_ref[...] = total[0:1] + total[1:2] + total[2:3]
 
 
-def params():
-    return pltpu.CompilerParams(vmem_limit_bytes=VMEM_LIMIT)
+def params(mib):
+    return pltpu.CompilerParams(vmem_limit_bytes=mib * MIB)
 
 
 def vmem(count):
@@ -547,7 +547,7 @@
         out_shape=(jax.ShapeDtypeStruct((slots, 128), I16), jax.ShapeDtypeStruct((1, columns), I32)),
         in_specs=vmem(4),
         out_specs=tuple(vmem(2)),
-        compiler_params=params(),
+        compiler_params=params(16),
         name="pack",
     )(planck_source, absorber_path, cloud_depth, row(span_map))
     early_units = LEV // (2 * GROUP) * (columns // BLOCK)
@@ -563,7 +563,7 @@
             pltpu.VMEM((g_lw + g_sw, NTAB), BF16),
             pltpu.VMEM((NTAB, units * EARLY * BLOCK), BF16),
         ],
-        compiler_params=params(),
+        compiler_params=params(24),
         cost_estimate=pl.CostEstimate(
             flops=2 * (g_lw + g_sw) * NTAB * early_units * EARLY * BLOCK,
             bytes_accessed=4 * (g_lw + g_sw) * early_units * EARLY * BLOCK,
@@ -600,7 +600,7 @@
             pltpu.VMEM((2, g_lw + g_sw, EARLY * BLOCK), F32),
             pltpu.SemaphoreType.DMA((2,)),
         ],
-        compiler_params=params(),
+        compiler_params=params(48),
         name="radiation",
     )(
         recv.reshape(slots, 128),
@@ -618,16 +618,15 @@
         row(solar_weight),
     )
     home = lax.all_to_all(back.reshape(devices, CAP, 128), ("dyn", "col"), 0, 0, tiled=True)
-    place = jnp.stack([lax.axis_index("dyn"), lax.axis_index("col")]).astype(I32)
     heating_lw, heating_sw, surface = pl.pallas_call(
         home_kernel,
         out_shape=(jax.ShapeDtypeStruct((LEV, columns), F32),) * 2
         + (jax.ShapeDtypeStruct((1, columns // 2), F32),),
-        in_specs=vmem(2) + [pl.BlockSpec(memory_space=pltpu.SMEM)],
+        in_specs=vmem(2),
         out_specs=tuple(vmem(3)),
-        compiler_params=params(),
+        compiler_params=params(16),
         name="home",
-    )(home.reshape(slots, 128), slot, place)
+    )(home.reshape(slots, 128), slot)
     return (heating_lw, heating_sw, surface.reshape(-1))
 
 

time: 107 us -> 104 us (0.972)
  blocking collectives: 0 us -> 21.5 us
  waiting for transfers between devices: 14.8 us -> 2.15 us
  Pallas kernels: 69.4 us -> 56.8 us
  local copies, waits for them, and re-layouts: 1.6 us -> 10.4 us
  starting transfers between devices: 19.9 us -> 11.5 us
    all_to_all x0 -> x1, blocking collectives: none -> 21.5 us  [body(): lax.all_to_all(back.reshape(devices, CAP, 128), ('dyn', 'col'), 0, 0, til...]
    all_to_all x1 -> x0, waiting for transfers between devices: 13.4 us -> none  [body(): lax.all_to_all(back.reshape(devices, CAP, 128), ('dyn', 'col'), 0, 0, til...]
    unnamed x4 -> x40, local copies, waits for them, and re-layouts: 1.6 us -> 10.4 us
    all_to_all x1 -> x0, starting transfers between devices: 8.44 us -> none  [body(): lax.all_to_all(back.reshape(devices, CAP, 128), ('dyn', 'col'), 0, 0, til...]
    pallas_call x1, Pallas kernels: 12.7 us -> 5 us  [body(): pl.pallas_call(absorb_kernel, grid=(early_units // units,), out_shape=jax...]
    pallas_call x1, Pallas kernels: 49.9 us -> 47 us  [body(): pl.pallas_call(partial(radiation_kernel, owners), out_shape=jax.ShapeDtyp...]
  transfers between devices with their start and end apart: 2 -> 1, of which waited for: 2 -> 1; matrix products, arithmetic and copies ran while one was open for 1% -> 0% of each run, Pallas kernels for 12% -> 5%
where the time goes in v4:
time: 104 us; the launch traced here: 103 us
  Pallas kernels  56.8 us (55%)
  blocking collectives  21.5 us (21%)
  starting transfers between devices  11.5 us (11%)
  local copies, waits for them, and re-layouts  10.4 us (10%)
  waiting for transfers between devices  2.15 us (2%)
    pallas_call x1, Pallas kernels, body(): pl.pallas_call(partial(radiation_kernel, owners), out_shape=jax.ShapeDtyp...  47 us
    all_to_all x1, blocking collectives, body(): lax.all_to_all(back.reshape(devices, CAP, 128), ('dyn', 'col'), 0, 0, til...  21.5 us
    all_to_all x1, starting transfers between devices, body(): lax.all_to_all(send.reshape(devices, CAP, 128), ('dyn', 'col'), 0, 0, til...  11.5 us
    unnamed x40, local copies, waits for them, and re-layouts  10.4 us
    pallas_call x1, Pallas kernels, body(): pl.pallas_call(absorb_kernel, grid=(early_units // units,), out_shape=jax...  5 us
    pallas_call x1, Pallas kernels, body(): pl.pallas_call(home_kernel, out_shape=(jax.ShapeDtypeStruct((LEV, columns...  2.43 us
    pallas_call x1, Pallas kernels, body(): pl.pallas_call(pack_kernel, out_shape=(jax.ShapeDtypeStruct((slots, 128),...  2.36 us
    all_to_all x1, waiting for transfers between devices, body(): lax.all_to_all(send.reshape(devices, CAP, 128), ('dyn', 'col'), 0, 0, til...  2.15 us
  transfers between devices with their start and end apart: 1, of which 1 were waited for; matrix products, arithmetic and copies ran while one was open for 0% of the time, Pallas kernels for 5%

profile of v4, /device:TPU:1, one launch (start us, length us, event | category | flops | bytes accessed | tf_op | source)
XLA Modules:
  0.0 103.2 jit_solution(10184406749862428902)
XLA Ops:
  0.6 0.0 copy-start.4
  0.6 0.0 copy-start.2
  0.7 0.0 copy-start.6
  0.7 0.0 copy-start.8
  0.7 1.0 copy-done.9
  1.7 0.9 copy-done.10
  2.6 0.9 copy-done.11
  3.5 0.7 copy-done.12
  4.2 0.0 copy-start.17
  4.2 0.0 copy-start.18
  4.2 0.0 copy-start.19
  4.2 2.4 %pack.1 = (s16[2048,128]{1,0:T(8,128)(2,1)}, s32[1,1024]{1,0:T(1,128)S(1)}) custom-call(f32[32,1024]{1,0:T(8,128)S(1)} %copy-done.9, f32[32,1024]{1,0:T(8,128)S(1)} %copy-done.10, f32[32,1024]{1,0:T(8,128)S(1)} %copy-done.11, s32[1,1024]{1,0:T(1,128)S(1)} %bitcast.16), custom_call_target="tpu_custom_call" | custom-call | tf_op jit(solution)/shard_map/pack/pallas_call | solution.py:545
  6.6 11.5 %all-to-all-start = ((s16[128,16,128]{2,1,0:T(8,128)(2,1)}), s16[128,16,128]{2,1,0:T(8,128)(2,1)S(1)}, u32[]{:S(2)}, u32[]{:S(2)}) async-start(s16[128,16,128]{2,1,0:T(8,128)(2,1)} %bitcast.1), calls=%async_computation | async-start | bytes 1048576 | tf_op jit(solution)/shard_map/all_to_all | solution.py:574
  18.1 0.0 copy-start.1
  18.1 1.0 copy-done.1
  19.1 1.0 copy-done.3
  20.1 0.9 copy-done.5
  21.1 0.9 copy-done.7
  22.0 5.0 %absorb.1.pre_ref = f32[16,480,256]{2,1,0:T(8,128)S(1)} custom-call(s32[32,1024]{1,0:T(8,128)S(1)} %copy-done.7, bf16[4,32,1024]{2,1,0:T(8,128)(2,1)S(1)} %copy-done.5, bf16[256,896]{1,0:T(8,128)(2,1)S(1)} %copy-done.1, bf16[224,896]{1,0:T(8,128)(2,1)S(1)} %copy-done.3), custom_call_target="tpu_custom_call" | custom-call | flops 3523215360 | bytes 7864320 | tf_op jit(solution)/shard_map/absorb/pallas_call | solution.py:555
  27.0 3.0 %copy-done = f32[16,480,256]{2,1,0:T(8,128)} copy-done((f32[16,480,256]{2,1,0:T(8,128)}, f32[16,480,256]{2,1,0:T(8,128)S(1)}, u32[]{:S(2)}) %copy-start) | copy-done | bytes 7864344
  30.0 2.1 %all-to-all-done = s16[128,16,128]{2,1,0:T(8,128)(2,1)S(1)} async-done(((s16[128,16,128]{2,1,0:T(8,128)(2,1)}), s16[128,16,128]{2,1,0:T(8,128)(2,1)S(1)}, u32[]{:S(2)}, u32[]{:S(2)}) %all-to-all-start) | async-done | bytes 524320 | tf_op jit(solution)/shard_map/all_to_all | solution.py:574
  32.3 47.0 %radiation.1 = s16[2048,128]{1,0:T(8,128)(2,1)S(1)} custom-call(s16[2048,128]{1,0:T(8,128)(2,1)S(1)} %bitcast.13, f32[16,480,256]{2,1,0:T(8,128)} %copy-done, f32[1,1024]{1,0:T(1,128)S(1)} %bitcast.17, s32[32,1024]{1,0:T(8,128)S(1)} %copy-done.8, bf16[4,32,1024]{2,1,0:T(8,128)(2,1)S(1)} %copy-done.6, s32[1,1024]{1,0:T(1,128)S(1)} %bitcast.18, ...), custom_call_target="tpu_custom_call" | custom-call | tf_op jit(solution)/shard_map/radiation/pallas_call | solution.py:575
  79.2 21.5 %all_to_all.10 = s16[128,16,128]{2,1,0:T(8,128)(2,1)S(1)} all-to-all(s16[128,16,128]{2,1,0:T(8,128)(2,1)S(1)} %bitcast.14), channel_id=1, replica_groups=mesh['dyn'=8,'col'=16] {'dyn','col'}, dimensions={0} | all-to-all | bytes 1048576 | tf_op jit(solution)/shard_map/all_to_all | solution.py:620
  100.7 2.4 %home.1 = (f32[32,1024]{1,0:T(8,128)}, f32[32,1024]{1,0:T(8,128)}, f32[1,512]{1,0:T(1,128)}) custom-call(s16[2048,128]{1,0:T(8,128)(2,1)S(1)} %bitcast.15, s32[1,1024]{1,0:T(1,128)S(1)} %get-tuple-element.9.slot_ref), custom_call_target="tpu_custom_call" | custom-call | tf_op jit(solution)/shard_map/home/pallas_call | solution.py:621
  (23 shorter events, 0.0 us)
Async XLA Ops:
  0.6 31.5 %copy-start.4 = (bf16[224,896]{1,0:T(8,128)(2,1)S(1)}, bf16[224,896]{1,0:T(8,128)(2,1)}, u32[]{:S(2)}) copy-start(bf16[224,896]{1,0:T(8,128)(2,1)} %table_sw_ref.3) | copy-start | bytes 1204228
  0.6 31.5 %copy-start.2 = (bf16[256,896]{1,0:T(8,128)(2,1)S(1)}, bf16[256,896]{1,0:T(8,128)(2,1)}, u32[]{:S(2)}) copy-start(bf16[256,896]{1,0:T(8,128)(2,1)} %table_lw_ref.3) | copy-start | bytes 1376260
  0.7 31.5 %copy-start.6 = (bf16[4,32,1024]{2,1,0:T(8,128)(2,1)S(1)}, bf16[4,32,1024]{2,1,0:T(8,128)(2,1)}, u32[]{:S(2)}) copy-start(bf16[4,32,1024]{2,1,0:T(8,128)(2,1)} %weight_ref.3) | copy-start | bytes 786436
  0.7 31.5 %copy-start.8 = (s32[32,1024]{1,0:T(8,128)S(1)}, s32[32,1024]{1,0:T(8,128)}, u32[]{:S(2)}) copy-start(s32[32,1024]{1,0:T(8,128)} %index_ref.3) | copy-start | bytes 393220
  0.7 1.0 copy-start.9
  1.7 0.9 copy-start.10
  2.6 0.9 copy-start.11
  3.5 0.7 copy-start.12
  4.2 28.0 %copy-start.13 = (f32[1024]{0:T(1024)S(1)}, f32[1024]{0:T(1024)}, u32[]{:S(2)}) copy-start(f32[1024]{0:T(1024)} %param.19) | copy-start | bytes 12292
  4.2 28.0 %copy-start.14 = (s32[1024]{0:T(1024)S(1)}, s32[1024]{0:T(1024)}, u32[]{:S(2)}) copy-start(s32[1024]{0:T(1024)} %param.22) | copy-start | bytes 12292
  4.2 28.0 %copy-start.15 = (s32[1024]{0:T(1024)S(1)}, s32[1024]{0:T(1024)}, u32[]{:S(2)}) copy-start(s32[1024]{0:T(1024)} %param.23) | copy-start | bytes 12292
  4.2 28.0 %copy-start.16 = (f32[1024]{0:T(1024)S(1)}, f32[1024]{0:T(1024)}, u32[]{:S(2)}) copy-start(f32[1024]{0:T(1024)} %param.24) | copy-start | bytes 12292
  4.2 28.0 %copy-start.17 = (f32[1024]{0:T(1024)S(1)}, f32[1024]{0:T(1024)}, u32[]{:S(2)}) copy-start(f32[1024]{0:T(1024)} %param.25) | copy-start | bytes 12292
  4.2 28.0 %copy-start.18 = (f32[256]{0:T(256)S(1)}, f32[256]{0:T(256)}, u32[]{:S(2)}) copy-start(f32[256]{0:T(256)} %param.28) | copy-start | bytes 3076
  4.2 28.0 %copy-start.19 = (f32[224]{0:T(256)S(1)}, f32[224]{0:T(256)}, u32[]{:S(2)}) copy-start(f32[224]{0:T(256)} %param.29) | copy-start | bytes 2692
  6.6 25.6 %all-to-all-start = ((s16[128,16,128]{2,1,0:T(8,128)(2,1)}), s16[128,16,128]{2,1,0:T(8,128)(2,1)S(1)}, u32[]{:S(2)}, u32[]{:S(2)}) async-start(s16[128,16,128]{2,1,0:T(8,128)(2,1)} %bitcast.1), calls=%async_computation | async-start | bytes 1048576 | tf_op jit(solution)/shard_map/all_to_all | solution.py:574
  18.1 1.0 copy-start.1
  19.1 1.0 copy-start.3
  20.1 0.9 copy-start.5
  21.1 0.9 copy-start.7
  27.0 3.1 %copy-start = (f32[16,480,256]{2,1,0:T(8,128)}, f32[16,480,256]{2,1,0:T(8,128)S(1)}, u32[]{:S(2)}) copy-start(f32[16,480,256]{2,1,0:T(8,128)S(1)} %absorb.1.pre_ref) | copy-start | bytes 23592964

commit v5 on v4

--- a/solution.py
+++ b/solution.py
@@ -150,14 +150,14 @@
     recv_ref,
     pre_ref,
     surface_ref,
-    index_ref,
-    weight_ref,
+    index_hbm,
+    weight_hbm,
     sunlit_ref,
     slot_ref,
     cosine_ref,
     albedo_ref,
-    table_lw_ref,
-    table_sw_ref,
+    table_lw_hbm,
+    table_sw_hbm,
     frac_ref,
     solar_ref,
     back_ref,
@@ -181,11 +181,22 @@
     heat,
     gain,
     pre_buf,
+    index_ref,
+    weight_ref,
     pre_sem,
+    load_sem,
 ):
     columns = index_ref.shape[1]
     slots = recv_ref.shape[0]
-    g_lw, g_sw = table_lw_ref.shape[0], table_sw_ref.shape[0]
+    g_lw, g_sw = table_lw_hbm.shape[0], table_sw_hbm.shape[0]
+    loads = [
+        pltpu.make_async_copy(index_hbm, index_ref, load_sem.at[0]),
+        pltpu.make_async_copy(weight_hbm, weight_ref, load_sem.at[1]),
+        pltpu.make_async_copy(table_lw_hbm, table.at[pl.ds(0, g_lw), pl.ds(0, NTAB)], load_sem.at[2]),
+        pltpu.make_async_copy(table_sw_hbm, table.at[pl.ds(g_lw, g_sw), pl.ds(0, NTAB)], load_sem.at[3]),
+    ]
+    for load in loads:
+        load.start()
     g_all = g_lw + g_sw
     first_fetch = pltpu.make_async_copy(pre_ref.at[0], pre_buf.at[0], pre_sem.at[0])
     first_fetch.start()
@@ -207,11 +218,11 @@
     planck_ext[pl.ds(1, LEV), :] = planck
     planck_ext[pl.ds(LEV + 1, 1), :] = surface_ref[...]
     ratio[...] = cloud / path
+    for load in loads:
+        load.wait()
     for k in range(4):
         weights[pl.ds(k * LEV, LEV), :] = weight_ref[k].astype(F32)
     ones = jnp.where(iota((g_all, 128), 1) < 3, 1.0, 0.0).astype(BF16)
-    table[:g_lw, :NTAB] = table_lw_ref[...]
-    table[g_lw:, :NTAB] = table_sw_ref[...]
     table[:, NTAB:] = ones
     for mix in (mix_a, mix_b):
         mix[NTAB:, :] = jnp.zeros((KPAD - NTAB, mix.shape[1]), BF16)
@@ -379,9 +390,9 @@
             enter_down(q)
 
         upward(q - per_block)
+        upward(q + 1 - per_block)
         prepare(q + 1, mix_b, out_b, levels - EARLY)
         downward(q, out_a)
-        upward(q + 1 - per_block)
         prepare(jnp.minimum(q + 2, groups - 1), mix_a, out_a)
         downward(q + 1, out_b, i & 1)
         return 0
@@ -512,6 +523,10 @@
     return pltpu.CompilerParams(vmem_limit_bytes=mib * MIB)
 
 
+def hbm(count):
+    return [pl.BlockSpec(memory_space=pltpu.HBM)] * count
+
+
 def vmem(count):
     return [pl.BlockSpec(memory_space=pltpu.VMEM)] * count
 
@@ -547,7 +562,7 @@
         out_shape=(jax.ShapeDtypeStruct((slots, 128), I16), jax.ShapeDtypeStruct((1, columns), I32)),
         in_specs=vmem(4),
         out_specs=tuple(vmem(2)),
-        compiler_params=params(16),
+        compiler_params=params(60),
         name="pack",
     )(planck_source, absorber_path, cloud_depth, row(span_map))
     early_units = LEV // (2 * GROUP) * (columns // BLOCK)
@@ -563,7 +578,7 @@
             pltpu.VMEM((g_lw + g_sw, NTAB), BF16),
             pltpu.VMEM((NTAB, units * EARLY * BLOCK), BF16),
         ],
-        compiler_params=params(24),
+        compiler_params=params(60),
         cost_estimate=pl.CostEstimate(
             flops=2 * (g_lw + g_sw) * NTAB * early_units * EARLY * BLOCK,
             bytes_accessed=4 * (g_lw + g_sw) * early_units * EARLY * BLOCK,
@@ -575,7 +590,7 @@
     back = pl.pallas_call(
         partial(radiation_kernel, owners),
         out_shape=jax.ShapeDtypeStruct((slots, 128), I16),
-        in_specs=vmem(1) + [pl.BlockSpec(memory_space=pl.ANY)] + vmem(11),
+        in_specs=vmem(1) + hbm(1) + vmem(1) + hbm(2) + vmem(4) + hbm(2) + vmem(2),
         out_specs=vmem(1)[0],
         scratch_shapes=[
             pltpu.VMEM((3 * LEV, columns), F32),
@@ -598,9 +613,12 @@
             pltpu.VMEM((2 * LEV, columns), F32),
             pltpu.VMEM((8, columns), F32),
             pltpu.VMEM((2, g_lw + g_sw, EARLY * BLOCK), F32),
+            pltpu.VMEM((LEV, columns), I32),
+            pltpu.VMEM((4, LEV, columns), BF16),
             pltpu.SemaphoreType.DMA((2,)),
+            pltpu.SemaphoreType.DMA((4,)),
         ],
-        compiler_params=params(48),
+        compiler_params=params(50),
         name="radiation",
     )(
         recv.reshape(slots, 128),

time: 104 us -> 98.1 us (0.943)
  local copies, waits for them, and re-layouts: 10.4 us -> 0.06 us
  Pallas kernels: 56.8 us -> 61.2 us
  waiting for transfers between devices: 2.15 us -> 6.41 us
  blocking collectives: 21.5 us -> 17.9 us
    unnamed x40 -> x24, local copies, waits for them, and re-layouts: 10.4 us -> 0.06 us
    all_to_all x1, waiting for transfers between devices: 2.15 us -> 6.41 us  [body(): lax.all_to_all(send.reshape(devices, CAP, 128), ('dyn', 'col'), 0, 0, til...]
    all_to_all x1, blocking collectives: 21.5 us -> 17.9 us  [body(): lax.all_to_all(back.reshape(devices, CAP, 128), ('dyn', 'col'), 0, 0, til...]
    pallas_call x1, Pallas kernels: 5 us -> 7.67 us  [body(): pl.pallas_call(absorb_kernel, grid=(early_units // units,), out_shape=jax...]
    pallas_call x1, Pallas kernels: 2.36 us -> 3.47 us  [body(): pl.pallas_call(pack_kernel, out_shape=(jax.ShapeDtypeStruct((slots, 128),...]
  transfers between devices with their start and end apart: 1 -> 1, of which waited for: 1 -> 1; matrix products, arithmetic and copies ran while one was open for 0% -> 0% of each run, Pallas kernels for 5% -> 8%
where the time goes in v5:
time: 98.1 us; the launch traced here: 97.9 us
  Pallas kernels  61.2 us (62%)
  blocking collectives  17.9 us (18%)
  starting transfers between devices  11.5 us (12%)
  waiting for transfers between devices  6.41 us (7%)
    pallas_call x1, Pallas kernels, body(): pl.pallas_call(partial(radiation_kernel, owners), out_shape=jax.ShapeDtyp...  47.7 us
    all_to_all x1, blocking collectives, body(): lax.all_to_all(back.reshape(devices, CAP, 128), ('dyn', 'col'), 0, 0, til...  17.9 us
    all_to_all x1, starting transfers between devices, body(): lax.all_to_all(send.reshape(devices, CAP, 128), ('dyn', 'col'), 0, 0, til...  11.5 us
    pallas_call x1, Pallas kernels, body(): pl.pallas_call(absorb_kernel, grid=(early_units // units,), out_shape=jax...  7.67 us
    all_to_all x1, waiting for transfers between devices, body(): lax.all_to_all(send.reshape(devices, CAP, 128), ('dyn', 'col'), 0, 0, til...  6.41 us
    pallas_call x1, Pallas kernels, body(): pl.pallas_call(pack_kernel, out_shape=(jax.ShapeDtypeStruct((slots, 128),...  3.47 us
    pallas_call x1, Pallas kernels, body(): pl.pallas_call(home_kernel, out_shape=(jax.ShapeDtypeStruct((LEV, columns...  2.43 us
  transfers between devices with their start and end apart: 1, of which 1 were waited for; matrix products, arithmetic and copies ran while one was open for 0% of the time, Pallas kernels for 8%

profile of v5, /device:TPU:1, one launch (start us, length us, event | category | flops | bytes accessed | tf_op | source)
XLA Modules:
  0.0 97.9 jit_solution(6494677865385221069)
XLA Ops:
  0.6 0.0 copy-start.1
  0.6 0.0 copy-start
  0.7 0.0 copy-start.2
  0.7 0.0 copy-start.3
  0.7 0.0 copy-start.11
  0.7 0.0 copy-start.10
  0.7 0.0 copy-start.8
  0.7 0.0 copy-start.7
  0.8 3.5 %pack.1 = (s16[2048,128]{1,0:T(8,128)(2,1)}, s32[1,1024]{1,0:T(1,128)}) custom-call(f32[32,1024]{1,0:T(8,128)} %planck_ref.1, f32[32,1024]{1,0:T(8,128)} %path_ref.1, f32[32,1024]{1,0:T(8,128)} %cloud_ref.1, s32[1,1024]{1,0:T(1,128)} %bitcast.24), custom_call_target="tpu_custom_call" | custom-call | tf_op jit(solution)/shard_map/pack/pallas_call | solution.py:560
  4.2 11.5 %all-to-all-start = ((s16[128,16,128]{2,1,0:T(8,128)(2,1)}), s16[128,16,128]{2,1,0:T(8,128)(2,1)S(1)}, u32[]{:S(2)}, u32[]{:S(2)}) async-start(s16[128,16,128]{2,1,0:T(8,128)(2,1)} %bitcast.23), calls=%async_computation | async-start | bytes 1048576 | tf_op jit(solution)/shard_map/all_to_all | solution.py:589
  15.7 7.7 %absorb.1.pre_ref = f32[16,480,256]{2,1,0:T(8,128)} custom-call(s32[32,1024]{1,0:T(8,128)} %index_hbm.1, bf16[4,32,1024]{2,1,0:T(8,128)(2,1)} %weight_hbm.1, bf16[256,896]{1,0:T(8,128)(2,1)} %table_lw_hbm.1, bf16[224,896]{1,0:T(8,128)(2,1)} %table_sw_hbm.1), custom_call_target="tpu_custom_call" | custom-call | flops 3523215360 | bytes 7864320 | tf_op jit(solution)/shard_map/absorb/pallas_call | solution.py:570
  23.4 6.4 %all-to-all-done = s16[128,16,128]{2,1,0:T(8,128)(2,1)S(1)} async-done(((s16[128,16,128]{2,1,0:T(8,128)(2,1)}), s16[128,16,128]{2,1,0:T(8,128)(2,1)S(1)}, u32[]{:S(2)}, u32[]{:S(2)}) %all-to-all-start) | async-done | bytes 524320 | tf_op jit(solution)/shard_map/all_to_all | solution.py:589
  29.8 0.0 copy-done.3
  29.8 0.0 copy-done.11
  29.8 0.0 copy-done.10
  29.8 0.0 copy-done.8
  29.9 0.0 copy-done.7
  29.9 0.0 copy-done.6
  29.9 0.0 copy-done.5
  29.9 0.0 copy-done.4
  29.9 47.7 %radiation.1 = s16[2048,128]{1,0:T(8,128)(2,1)S(1)} custom-call(s16[2048,128]{1,0:T(8,128)(2,1)S(1)} %bitcast.13, f32[16,480,256]{2,1,0:T(8,128)} %absorb.1.pre_ref, f32[1,1024]{1,0:T(1,128)S(1)} %bitcast.16, s32[32,1024]{1,0:T(8,128)S(1)} %copy-done.3, bf16[4,32,1024]{2,1,0:T(8,128)(2,1)S(1)} %copy-done.2, s32[1,1024]{1,0:T(1,128)S(1)} %bitcast.17, ...), custom_call_target="tpu_custom_call" | custom-call | tf_op jit(solution)/shard_map/radiation/pallas_call | solution.py:590
  77.6 17.9 %all_to_all.10 = s16[128,16,128]{2,1,0:T(8,128)(2,1)S(1)} all-to-all(s16[128,16,128]{2,1,0:T(8,128)(2,1)S(1)} %bitcast.14), channel_id=1, replica_groups=mesh['dyn'=8,'col'=16] {'dyn','col'}, dimensions={0} | all-to-all | bytes 1048576 | tf_op jit(solution)/shard_map/all_to_all | solution.py:638
  95.4 0.0 copy-done.9
  95.4 2.4 %home.1 = (f32[32,1024]{1,0:T(8,128)}, f32[32,1024]{1,0:T(8,128)}, f32[1,512]{1,0:T(1,128)}) custom-call(s16[2048,128]{1,0:T(8,128)(2,1)S(1)} %bitcast.15, s32[1,1024]{1,0:T(1,128)S(1)} %copy-done.9), custom_call_target="tpu_custom_call" | custom-call | tf_op jit(solution)/shard_map/home/pallas_call | solution.py:639
  (7 shorter events, 0.0 us)
Async XLA Ops:
  0.6 29.2 %copy-start.1 = (bf16[224,896]{1,0:T(8,128)(2,1)S(1)}, bf16[224,896]{1,0:T(8,128)(2,1)}, u32[]{:S(2)}) copy-start(bf16[224,896]{1,0:T(8,128)(2,1)} %table_sw_hbm.1) | copy-start | bytes 1204228
  0.6 29.2 %copy-start = (bf16[256,896]{1,0:T(8,128)(2,1)S(1)}, bf16[256,896]{1,0:T(8,128)(2,1)}, u32[]{:S(2)}) copy-start(bf16[256,896]{1,0:T(8,128)(2,1)} %table_lw_hbm.1) | copy-start | bytes 1376260
  0.7 29.2 %copy-start.2 = (bf16[4,32,1024]{2,1,0:T(8,128)(2,1)S(1)}, bf16[4,32,1024]{2,1,0:T(8,128)(2,1)}, u32[]{:S(2)}) copy-start(bf16[4,32,1024]{2,1,0:T(8,128)(2,1)} %weight_hbm.1) | copy-start | bytes 786436
  0.7 29.1 %copy-start.3 = (s32[32,1024]{1,0:T(8,128)S(1)}, s32[32,1024]{1,0:T(8,128)}, u32[]{:S(2)}) copy-start(s32[32,1024]{1,0:T(8,128)} %index_hbm.1) | copy-start | bytes 393220
  0.7 29.1 %copy-start.11 = (f32[224]{0:T(256)S(1)}, f32[224]{0:T(256)}, u32[]{:S(2)}) copy-start(f32[224]{0:T(256)} %param.29) | copy-start | bytes 2692
  0.7 29.1 %copy-start.10 = (f32[256]{0:T(256)S(1)}, f32[256]{0:T(256)}, u32[]{:S(2)}) copy-start(f32[256]{0:T(256)} %param.28) | copy-start | bytes 3076
  0.7 29.1 %copy-start.8 = (f32[1024]{0:T(1024)S(1)}, f32[1024]{0:T(1024)}, u32[]{:S(2)}) copy-start(f32[1024]{0:T(1024)} %param.25) | copy-start | bytes 12292
  0.7 29.1 %copy-start.7 = (f32[1024]{0:T(1024)S(1)}, f32[1024]{0:T(1024)}, u32[]{:S(2)}) copy-start(f32[1024]{0:T(1024)} %param.24) | copy-start | bytes 12292
  0.7 29.1 %copy-start.6 = (s32[1024]{0:T(1024)S(1)}, s32[1024]{0:T(1024)}, u32[]{:S(2)}) copy-start(s32[1024]{0:T(1024)} %param.23) | copy-start | bytes 12292
  0.7 29.1 %copy-start.5 = (s32[1024]{0:T(1024)S(1)}, s32[1024]{0:T(1024)}, u32[]{:S(2)}) copy-start(s32[1024]{0:T(1024)} %param.22) | copy-start | bytes 12292
  0.7 29.1 %copy-start.4 = (f32[1024]{0:T(1024)S(1)}, f32[1024]{0:T(1024)}, u32[]{:S(2)}) copy-start(f32[1024]{0:T(1024)} %param.19) | copy-start | bytes 12292
  4.2 25.6 %all-to-all-start = ((s16[128,16,128]{2,1,0:T(8,128)(2,1)}), s16[128,16,128]{2,1,0:T(8,128)(2,1)S(1)}, u32[]{:S(2)}, u32[]{:S(2)}) async-start(s16[128,16,128]{2,1,0:T(8,128)(2,1)} %bitcast.23), calls=%async_computation | async-start | bytes 1048576 | tf_op jit(solution)/shard_map/all_to_all | solution.py:589
  23.4 72.1 %copy-start.9 = (s32[1,1024]{1,0:T(1,128)S(1)}, s32[1,1024]{1,0:T(1,128)}, u32[]{:S(2)}) copy-start(s32[1,1024]{1,0:T(1,128)} %get-tuple-element.9.slot_ref) | copy-start | bytes 12292

commit v6 on v4

--- a/solution.py
+++ b/solution.py
@@ -379,9 +379,9 @@
             enter_down(q)
 
         upward(q - per_block)
+        upward(q + 1 - per_block)
         prepare(q + 1, mix_b, out_b, levels - EARLY)
         downward(q, out_a)
-        upward(q + 1 - per_block)
         prepare(jnp.minimum(q + 2, groups - 1), mix_a, out_a)
         downward(q + 1, out_b, i & 1)
         return 0
@@ -547,7 +547,7 @@
         out_shape=(jax.ShapeDtypeStruct((slots, 128), I16), jax.ShapeDtypeStruct((1, columns), I32)),
         in_specs=vmem(4),
         out_specs=tuple(vmem(2)),
-        compiler_params=params(16),
+        compiler_params=params(60),
         name="pack",
     )(planck_source, absorber_path, cloud_depth, row(span_map))
     early_units = LEV // (2 * GROUP) * (columns // BLOCK)
@@ -563,7 +563,7 @@
             pltpu.VMEM((g_lw + g_sw, NTAB), BF16),
             pltpu.VMEM((NTAB, units * EARLY * BLOCK), BF16),
         ],
-        compiler_params=params(24),
+        compiler_params=params(60),
         cost_estimate=pl.CostEstimate(
             flops=2 * (g_lw + g_sw) * NTAB * early_units * EARLY * BLOCK,
             bytes_accessed=4 * (g_lw + g_sw) * early_units * EARLY * BLOCK,
@@ -600,7 +600,7 @@
             pltpu.VMEM((2, g_lw + g_sw, EARLY * BLOCK), F32),
             pltpu.SemaphoreType.DMA((2,)),
         ],
-        compiler_params=params(48),
+        compiler_params=params(50),
         name="radiation",
     )(
         recv.reshape(slots, 128),

time: 104 us -> 97.7 us (0.939)
  local copies, waits for them, and re-layouts: 10.4 us -> 0.06 us
  waiting for transfers between devices: 2.15 us -> 6.41 us
  Pallas kernels: 56.8 us -> 60.8 us
  blocking collectives: 21.5 us -> 17.9 us
    unnamed x40 -> x24, local copies, waits for them, and re-layouts: 10.4 us -> 0.06 us
    all_to_all x1, waiting for transfers between devices: 2.15 us -> 6.41 us  [body(): lax.all_to_all(send.reshape(devices, CAP, 128), ('dyn', 'col'), 0, 0, til...]
    all_to_all x1, blocking collectives: 21.5 us -> 17.9 us  [body(): lax.all_to_all(back.reshape(devices, CAP, 128), ('dyn', 'col'), 0, 0, til...]
    pallas_call x1, Pallas kernels: 5 us -> 7.67 us  [body(): pl.pallas_call(absorb_kernel, grid=(early_units // units,), out_shape=jax...]
    pallas_call x1, Pallas kernels: 2.36 us -> 3.47 us  [body(): pl.pallas_call(pack_kernel, out_shape=(jax.ShapeDtypeStruct((slots, 128),...]
  transfers between devices with their start and end apart: 1 -> 1, of which waited for: 1 -> 1; matrix products, arithmetic and copies ran while one was open for 0% -> 0% of each run, Pallas kernels for 5% -> 8%
where the time goes in v6:
time: 97.7 us; the launch traced here: 97.5 us
  Pallas kernels  60.8 us (62%)
  blocking collectives  17.9 us (18%)
  starting transfers between devices  11.5 us (12%)
  waiting for transfers between devices  6.41 us (7%)
    pallas_call x1, Pallas kernels, body(): pl.pallas_call(partial(radiation_kernel, owners), out_shape=jax.ShapeDtyp...  47.3 us
    all_to_all x1, blocking collectives, body(): lax.all_to_all(back.reshape(devices, CAP, 128), ('dyn', 'col'), 0, 0, til...  17.9 us
    all_to_all x1, starting transfers between devices, body(): lax.all_to_all(send.reshape(devices, CAP, 128), ('dyn', 'col'), 0, 0, til...  11.5 us
    pallas_call x1, Pallas kernels, body(): pl.pallas_call(absorb_kernel, grid=(early_units // units,), out_shape=jax...  7.67 us
    all_to_all x1, waiting for transfers between devices, body(): lax.all_to_all(send.reshape(devices, CAP, 128), ('dyn', 'col'), 0, 0, til...  6.41 us
    pallas_call x1, Pallas kernels, body(): pl.pallas_call(pack_kernel, out_shape=(jax.ShapeDtypeStruct((slots, 128),...  3.47 us
    pallas_call x1, Pallas kernels, body(): pl.pallas_call(home_kernel, out_shape=(jax.ShapeDtypeStruct((LEV, columns...  2.43 us
  transfers between devices with their start and end apart: 1, of which 1 were waited for; matrix products, arithmetic and copies ran while one was open for 0% of the time, Pallas kernels for 8%

profile of v6, /device:TPU:1, one launch (start us, length us, event | category | flops | bytes accessed | tf_op | source)
XLA Modules:
  0.0 97.5 jit_solution(14619522245033355966)
XLA Ops:
  0.6 0.0 copy-start.1
  0.6 0.0 copy-start
  0.7 0.0 copy-start.2
  0.7 0.0 copy-start.3
  0.7 0.0 copy-start.11
  0.7 0.0 copy-start.10
  0.7 0.0 copy-start.8
  0.7 0.0 copy-start.7
  0.7 0.0 copy-start.6
  0.7 0.0 copy-start.5
  0.7 0.0 copy-start.4
  0.8 3.5 %pack.1 = (s16[2048,128]{1,0:T(8,128)(2,1)}, s32[1,1024]{1,0:T(1,128)}) custom-call(f32[32,1024]{1,0:T(8,128)} %planck_ref.1, f32[32,1024]{1,0:T(8,128)} %path_ref.1, f32[32,1024]{1,0:T(8,128)} %cloud_ref.1, s32[1,1024]{1,0:T(1,128)} %bitcast.24), custom_call_target="tpu_custom_call" | custom-call | tf_op jit(solution)/shard_map/pack/pallas_call | solution.py:545
  4.2 11.5 %all-to-all-start = ((s16[128,16,128]{2,1,0:T(8,128)(2,1)}), s16[128,16,128]{2,1,0:T(8,128)(2,1)S(1)}, u32[]{:S(2)}, u32[]{:S(2)}) async-start(s16[128,16,128]{2,1,0:T(8,128)(2,1)} %bitcast.23), calls=%async_computation | async-start | bytes 1048576 | tf_op jit(solution)/shard_map/all_to_all | solution.py:574
  15.7 7.7 %absorb.1.pre_ref = f32[16,480,256]{2,1,0:T(8,128)} custom-call(s32[32,1024]{1,0:T(8,128)} %index_ref.3, bf16[4,32,1024]{2,1,0:T(8,128)(2,1)} %weight_ref.3, bf16[256,896]{1,0:T(8,128)(2,1)} %table_lw_ref.3, bf16[224,896]{1,0:T(8,128)(2,1)} %table_sw_ref.3), custom_call_target="tpu_custom_call" | custom-call | flops 3523215360 | bytes 7864320 | tf_op jit(solution)/shard_map/absorb/pallas_call | solution.py:555
  23.4 6.4 %all-to-all-done = s16[128,16,128]{2,1,0:T(8,128)(2,1)S(1)} async-done(((s16[128,16,128]{2,1,0:T(8,128)(2,1)}), s16[128,16,128]{2,1,0:T(8,128)(2,1)S(1)}, u32[]{:S(2)}, u32[]{:S(2)}) %all-to-all-start) | async-done | bytes 524320 | tf_op jit(solution)/shard_map/all_to_all | solution.py:574
  29.8 0.0 copy-done.1
  29.8 0.0 copy-done
  29.8 0.0 copy-done.2
  29.8 0.0 copy-done.3
  29.8 0.0 copy-done.11
  29.8 0.0 copy-done.10
  29.9 47.3 %radiation.1 = s16[2048,128]{1,0:T(8,128)(2,1)S(1)} custom-call(s16[2048,128]{1,0:T(8,128)(2,1)S(1)} %bitcast.13, f32[16,480,256]{2,1,0:T(8,128)} %absorb.1.pre_ref, f32[1,1024]{1,0:T(1,128)S(1)} %bitcast.16, s32[32,1024]{1,0:T(8,128)S(1)} %copy-done.3, bf16[4,32,1024]{2,1,0:T(8,128)(2,1)S(1)} %copy-done.2, s32[1,1024]{1,0:T(1,128)S(1)} %bitcast.17, ...), custom_call_target="tpu_custom_call" | custom-call | tf_op jit(solution)/shard_map/radiation/pallas_call | solution.py:575
  77.2 17.9 %all_to_all.10 = s16[128,16,128]{2,1,0:T(8,128)(2,1)S(1)} all-to-all(s16[128,16,128]{2,1,0:T(8,128)(2,1)S(1)} %bitcast.14), channel_id=1, replica_groups=mesh['dyn'=8,'col'=16] {'dyn','col'}, dimensions={0} | all-to-all | bytes 1048576 | tf_op jit(solution)/shard_map/all_to_all | solution.py:620
  95.0 2.4 %home.1 = (f32[32,1024]{1,0:T(8,128)}, f32[32,1024]{1,0:T(8,128)}, f32[1,512]{1,0:T(1,128)}) custom-call(s16[2048,128]{1,0:T(8,128)(2,1)S(1)} %bitcast.15, s32[1,1024]{1,0:T(1,128)S(1)} %copy-done.9), custom_call_target="tpu_custom_call" | custom-call | tf_op jit(solution)/shard_map/home/pallas_call | solution.py:621
  (7 shorter events, 0.0 us)
Async XLA Ops:
  0.6 29.2 %copy-start.1 = (bf16[224,896]{1,0:T(8,128)(2,1)S(1)}, bf16[224,896]{1,0:T(8,128)(2,1)}, u32[]{:S(2)}) copy-start(bf16[224,896]{1,0:T(8,128)(2,1)} %table_sw_ref.3) | copy-start | bytes 1204228
  0.6 29.2 %copy-start = (bf16[256,896]{1,0:T(8,128)(2,1)S(1)}, bf16[256,896]{1,0:T(8,128)(2,1)}, u32[]{:S(2)}) copy-start(bf16[256,896]{1,0:T(8,128)(2,1)} %table_lw_ref.3) | copy-start | bytes 1376260
  0.7 29.2 %copy-start.2 = (bf16[4,32,1024]{2,1,0:T(8,128)(2,1)S(1)}, bf16[4,32,1024]{2,1,0:T(8,128)(2,1)}, u32[]{:S(2)}) copy-start(bf16[4,32,1024]{2,1,0:T(8,128)(2,1)} %weight_ref.3) | copy-start | bytes 786436
  0.7 29.1 %copy-start.3 = (s32[32,1024]{1,0:T(8,128)S(1)}, s32[32,1024]{1,0:T(8,128)}, u32[]{:S(2)}) copy-start(s32[32,1024]{1,0:T(8,128)} %index_ref.3) | copy-start | bytes 393220
  0.7 29.1 %copy-start.11 = (f32[224]{0:T(256)S(1)}, f32[224]{0:T(256)}, u32[]{:S(2)}) copy-start(f32[224]{0:T(256)} %param.29) | copy-start | bytes 2692
  0.7 29.1 %copy-start.10 = (f32[256]{0:T(256)S(1)}, f32[256]{0:T(256)}, u32[]{:S(2)}) copy-start(f32[256]{0:T(256)} %param.28) | copy-start | bytes 3076
  0.7 29.1 %copy-start.8 = (f32[1024]{0:T(1024)S(1)}, f32[1024]{0:T(1024)}, u32[]{:S(2)}) copy-start(f32[1024]{0:T(1024)} %param.25) | copy-start | bytes 12292
  0.7 29.1 %copy-start.7 = (f32[1024]{0:T(1024)S(1)}, f32[1024]{0:T(1024)}, u32[]{:S(2)}) copy-start(f32[1024]{0:T(1024)} %param.24) | copy-start | bytes 12292
  0.7 29.1 %copy-start.6 = (s32[1024]{0:T(1024)S(1)}, s32[1024]{0:T(1024)}, u32[]{:S(2)}) copy-start(s32[1024]{0:T(1024)} %param.23) | copy-start | bytes 12292
  0.7 29.1 %copy-start.5 = (s32[1024]{0:T(1024)S(1)}, s32[1024]{0:T(1024)}, u32[]{:S(2)}) copy-start(s32[1024]{0:T(1024)} %param.22) | copy-start | bytes 12292
  0.7 29.1 %copy-start.4 = (f32[1024]{0:T(1024)S(1)}, f32[1024]{0:T(1024)}, u32[]{:S(2)}) copy-start(f32[1024]{0:T(1024)} %param.19) | copy-start | bytes 12292
  4.2 25.6 %all-to-all-start = ((s16[128,16,128]{2,1,0:T(8,128)(2,1)}), s16[128,16,128]{2,1,0:T(8,128)(2,1)S(1)}, u32[]{:S(2)}, u32[]{:S(2)}) async-start(s16[128,16,128]{2,1,0:T(8,128)(2,1)} %bitcast.23), calls=%async_computation | async-start | bytes 1048576 | tf_op jit(solution)/shard_map/all_to_all | solution.py:574
  23.4 71.6 %copy-start.9 = (s32[1,1024]{1,0:T(1,128)S(1)}, s32[1,1024]{1,0:T(1,128)}, u32[]{:S(2)}) copy-start(s32[1,1024]{1,0:T(1,128)} %get-tuple-element.9.slot_ref) | copy-start | bytes 12292
